TPU v7x, 128 devices: a whole 4x4x4 slice. The times are simulated.
128 devices in a mesh: seq: 16 (over y_lo, x, core), aud: 8 (over y_hi, z).
Axes of the slice: x: 4, y: 4 (y_hi: 2, y_lo: 2; y = y_hi * 2 + y_lo), z: 4, core: 2. Of those that a mesh axis runs over, the one named last changes fastest.
Arguments:
- video_q: bfloat16 [8192, 3072], P('seq', 'aud'), may hold values from -18 to 18
- video_k: bfloat16 [8192, 3072], P('seq', 'aud'), may hold values from -4.5 to 4.5
- video_v: bfloat16 [8192, 3072], P('seq', 'aud'), may hold values from -6 to 6
- audio_k: bfloat16 [512, 3072], P('aud'), may hold values from -4.5 to 4.5
- audio_v: bfloat16 [512, 3072], P('aud'), may hold values from -6 to 6
- text_k: bfloat16 [512, 3072], P('seq', 'aud'), may hold values from -4.5 to 4.5
- text_v: bfloat16 [512, 3072], P('seq', 'aud'), may hold values from -6 to 6
- block_start: int32 [64], P('seq'), may hold values from 0 to 510, as said below
- block_len: int32 [64], P('seq'), may hold values from 2 to 128, as said below
- prompt_len: int32 [1], replicated, may hold values from 128 to 512
- w_out: bfloat16 [3072, 3072], P('aud'), may hold values from -0.109375 to 0.109375
Outputs:
- video_out: bfloat16 [8192, 3072], P(('seq', 'aud'))
Inputs may be any that keep to these rules, and one draw needn't show every extreme that they name: block_start[b] + block_len[b] <= 512 for every block b; with c = b * 8 + 512 // 128, block b's window lies within audio tokens c - 128 to c + 128: block_start[b] >= c - 128 and block_start[b] + block_len[b] <= c + 128. `block_len`: some block's window holds exactly 128 audio tokens.
All inputs are finite; a program needn't handle non-finite values.
Results may differ from a plain program's by a relative error of at most 0.017.
Values may be sent and summed in bfloat16 or wider, within the bound.
No kernel may reach another device: no remote copies, remote signals or barrier semaphores. Data moves between devices by JAX's collectives and lax.ppermute only.
A program may use at most 128 MiB of HBM per device.

v0:
```python
import jax
import jax.numpy as jnp
from jax import lax
from jax.sharding import PartitionSpec as P

HD = 128
VBLK = 128
WIN = 128


def attend_block(running, queries, key_rows, value_rows, allowed):
    peak_score, weight_sum, weighted = running
    keys_split = key_rows.reshape(key_rows.shape[0], -1, HD)
    values_split = value_rows.reshape(value_rows.shape[0], -1, HD)
    scores = jnp.einsum(
        "qhd,khd->hqk", queries, keys_split, preferred_element_type=jnp.float32
    ) * HD ** (-0.5)
    if allowed is not None:
        scores = jnp.where(allowed[None, None, :] > 0, scores, -1e30)
    new_peak = jnp.maximum(peak_score, jnp.max(scores, axis=-1))
    weights = jnp.exp(scores - new_peak[..., None])
    rescale = jnp.exp(peak_score - new_peak)
    weight_sum = weight_sum * rescale + jnp.sum(weights, axis=-1)
    weighted = weighted * rescale[..., None] + jnp.einsum(
        "hqk,khd->hqd",
        weights.astype(jnp.bfloat16),
        values_split,
        preferred_element_type=jnp.float32,
    )
    return (new_peak, weight_sum, weighted)


def attend_keys(running, queries, key_rows, value_rows):
    key_count = key_rows.shape[0]
    key_blocks = key_rows.reshape(key_count // 512, 512, key_rows.shape[1])
    value_blocks = value_rows.reshape(key_count // 512, 512, value_rows.shape[1])

    def step(state, paired):
        return (attend_block(state, queries, paired[0], paired[1], None), None)

    running, unused = lax.scan(step, running, (key_blocks, value_blocks))
    return running


def finish(running, row_count):
    peak_score, weight_sum, weighted = running
    mixture = weighted / weight_sum[..., None]
    return jnp.transpose(mixture, (1, 0, 2)).reshape(row_count, -1)


def window_of(audio_table, offset):
    return lax.dynamic_slice_in_dim(audio_table, offset, WIN, 0)


def on_device(
    video_q,
    video_k,
    video_v,
    audio_k,
    audio_v,
    text_k,
    text_v,
    block_start,
    block_len,
    prompt_len,
    w_out,
):
    row_count = video_q.shape[0]
    queries = video_q.reshape(row_count, -1, HD)
    head_count = queries.shape[1]
    empty_state = (
        jnp.full((head_count, row_count), -jnp.inf, jnp.float32),
        jnp.zeros((head_count, row_count), jnp.float32),
        jnp.zeros((head_count, row_count, HD), jnp.float32),
    )
    text_count = text_k.shape[0]
    positions = lax.axis_index("seq") * text_count + jnp.arange(text_count, dtype=jnp.int32)
    text_live = (positions < prompt_len[0]).astype(jnp.bfloat16)
    incoming = (
        lax.all_gather(video_k, "seq", axis=0, tiled=True),
        lax.all_gather(video_v, "seq", axis=0, tiled=True),
    )
    video_state = attend_keys(empty_state, queries, incoming[0], incoming[1])
    incoming = (
        lax.all_gather(text_k, "seq", axis=0, tiled=True),
        lax.all_gather(text_v, "seq", axis=0, tiled=True),
        lax.all_gather(text_live, "seq", axis=0, tiled=True),
    )
    text_state = attend_block(empty_state, queries, incoming[0], incoming[1], incoming[2])
    audio_keys, audio_vals = (
        lax.all_to_all(audio_k, "aud", split_axis=1, concat_axis=0, tiled=True),
        lax.all_to_all(audio_v, "aud", split_axis=1, concat_axis=0, tiled=True),
    )
    audio_span = audio_keys.shape[0]
    block_count = row_count // VBLK
    offsets = jnp.minimum(block_start, audio_span - WIN)
    near_keys = jax.vmap(window_of, in_axes=(None, 0))(audio_keys, offsets).reshape(
        block_count, WIN, head_count, HD
    )
    near_vals = jax.vmap(window_of, in_axes=(None, 0))(audio_vals, offsets).reshape(
        block_count, WIN, head_count, HD
    )
    key_index = offsets[:, None] + jnp.arange(WIN, dtype=jnp.int32)[None, :]
    inside = (key_index >= block_start[:, None]) & (key_index < (block_start + block_len)[:, None])
    block_q = queries.reshape(block_count, VBLK, head_count, HD)
    scores = jnp.einsum(
        "bqhd,bkhd->bhqk", block_q, near_keys, preferred_element_type=jnp.float32
    ) * HD ** (-0.5)
    scores = jnp.where(inside[:, None, None, :], scores, -1e30)
    weights = jnp.exp(scores - jnp.max(scores, axis=-1, keepdims=True))
    weight_sum = jnp.sum(weights, axis=-1)
    heard = jnp.einsum(
        "bhqk,bkhd->bhqd",
        weights.astype(jnp.bfloat16),
        near_vals,
        preferred_element_type=jnp.float32,
    )
    heard = heard / weight_sum[..., None]
    audio_part = jnp.transpose(heard, (0, 2, 1, 3)).reshape(row_count, -1)
    self_part = finish(video_state, row_count)
    text_part = finish(text_state, row_count)
    joined_heads = (self_part + audio_part + text_part).astype(jnp.bfloat16)
    return lax.psum_scatter(
        jnp.dot(joined_heads, w_out, preferred_element_type=jnp.float32).astype(jnp.bfloat16),
        "aud",
        scatter_dimension=0,
        tiled=True,
    )


def solution(mesh):
    placed = (
        P("seq", "aud"),
        P("seq", "aud"),
        P("seq", "aud"),
        P("aud", None),
        P("aud", None),
        P("seq", "aud"),
        P("seq", "aud"),
        P("seq"),
        P("seq"),
        P(),
        P("aud", None),
    )
    return jax.shard_map(
        on_device, mesh=mesh, in_specs=placed, out_specs=P(("seq", "aud"), None), check_vma=False
    )
```

profile of v0, /device:TPU:1, one launch (start us, length us, event | category | flops | bytes accessed | tf_op | source)
XLA Modules:
  0.0 413.9 jit_solution(14755843736944083968)
XLA Ops:
  9.8 8.5 %all-to-all-start = ((bf16[64,8,384]{2,0,1:T(8,128)(2,1)}), bf16[64,8,384]{2,0,1:T(8,128)(2,1)S(1)}, u32[]{:S(2)}, u32[]{:S(2)}) async-start(bf16[64,8,384]{2,0,1:T(8,128)(2,1)} %bitcast.89), calls=%async_computation | async-start | bytes 786432 | tf_op jit(solution)/shard_map/all_to_all | solution.py:91
  25.1 21.3 %all_gather.19 = bf16[512,384]{1,0:T(8,128)(2,1)S(1)} all-gather(bf16[32,384]{1,0:T(8,128)(2,1)} %param.19), channel_id=1, replica_groups=mesh['seq'=16,'aud'=8] {'seq'}, dimensions={0}, use_global_device_ids=true | all-gather | bytes 417792 | tf_op jit(solution)/shard_map/all_gather | solution.py:86
  48.0 19.0 %all_gather.18 = bf16[512,384]{1,0:T(8,128)(2,1)} all-gather(bf16[32,384]{1,0:T(8,128)(2,1)} %param.18), channel_id=1, replica_groups=mesh['seq'=16,'aud'=8] {'seq'}, dimensions={0}, use_global_device_ids=true | all-gather | bytes 417792 | tf_op jit(solution)/shard_map/all_gather | solution.py:85
  72.5 28.0 %all-reduce.1 = bf16[512]{0:T(512)(128)(2,1)} all-reduce(bf16[512]{0:T(512)(128)(2,1)} %dynamic-update-slice.4), channel_id=1, replica_groups=mesh['seq'=16,'aud'=8] {'seq'}, use_global_device_ids=true, to_apply=%add.1 | all-reduce | flops 512 | bytes 2048
  105.9 7.6 %all-to-all-start.1 = ((bf16[64,8,384]{2,0,1:T(8,128)(2,1)}), bf16[64,8,384]{2,0,1:T(8,128)(2,1)}, u32[]{:S(2)}, u32[]{:S(2)}) async-start(bf16[64,8,384]{2,0,1:T(8,128)(2,1)} %bitcast.88), calls=%async_computation.1 | async-start | bytes 786432 | tf_op jit(solution)/shard_map/all_to_all | solution.py:92
  113.5 6.3 %while.17 = (s32[]{:T(128)}, bf16[512,384]{1,0:T(8,128)(2,1)S(1)}, s32[4,2]{0,1:T(2,128)S(1)}, bf16[4,128,384]{1,2,0:T(8,128)(2,1)S(1)}, s32[]{:T(128)}) while((s32[]{:T(128)}, bf16[512,384]{1,0:T(8,128)(2,1)S(1)}, s32[4,2]{0,1:T(2,128)S(1)}, bf16[4,128,384]{1,2,0:T(8,128)(2,1)S(1)}, s32[]{:T(128)}) %tuple.78), condition=%wide.while_cond, body=%wide.while_body.sunk | while | flops 2 | bytes 589929 | solution.py:52
  122.9 15.0 %while.18 = (s32[]{:T(128)}, bf16[512,384]{1,0:T(8,128)(2,1)}, s32[4,2]{0,1:T(2,128)}, bf16[4,128,384]{1,2,0:T(8,128)(2,1)}, s32[]{:T(128)}) while((s32[]{:T(128)}, bf16[512,384]{1,0:T(8,128)(2,1)}, s32[4,2]{0,1:T(2,128)}, bf16[4,128,384]{1,2,0:T(8,128)(2,1)}, s32[]{:T(128)}) %tuple.60), condition=%wide.while_cond.1, body=%wide.while_body.1.sunk | while | flops 2 | bytes 589929 | solution.py:52
  142.5 178.9 %while.19 = (s32[]{:T(128)}, f32[3,512]{1,0:T(4,128)S(1)}, f32[3,512]{1,0:T(4,128)S(1)}, f32[3,512,128]{2,1,0:T(8,128)}, bf16[16,512,384]{2,1,0:T(8,128)(2,1)}, ...) while((s32[]{:T(128)}, f32[3,512]{1,0:T(4,128)S(1)}, ...), condition=%wide.region_3.4_spmd.clone, body=%wide.region_0.3_spmd.clone.sunk | while | flops 409542144 | bytes 15433845 | solution.py:41
  143.9 3.3 bitcast_reduce_fusion.2
  147.2 2.4 fusion.68
  149.8 3.7 fusion.70
  154.9 3.3 bitcast_reduce_fusion.2
  158.2 2.4 fusion.68
  160.8 3.9 fusion.70
  166.1 3.3 bitcast_reduce_fusion.2
  169.4 2.4 fusion.68
  172.0 3.9 fusion.70
  177.3 3.3 bitcast_reduce_fusion.2
  180.6 2.4 fusion.68
  183.2 3.9 fusion.70
  188.5 3.3 bitcast_reduce_fusion.2
  191.8 2.4 fusion.68
  194.4 3.9 fusion.70
  199.7 3.3 bitcast_reduce_fusion.2
  202.9 2.4 fusion.68
  205.6 3.9 fusion.70
  210.9 3.3 bitcast_reduce_fusion.2
  216.8 3.9 fusion.70
  222.1 3.3 bitcast_reduce_fusion.2
  228.0 3.9 fusion.70
  233.2 3.3 bitcast_reduce_fusion.2
  239.2 3.9 fusion.70
  244.4 3.3 bitcast_reduce_fusion.2
  250.4 3.9 fusion.70
  255.6 3.3 bitcast_reduce_fusion.2
  261.5 3.9 fusion.70
  266.8 3.3 bitcast_reduce_fusion.2
  272.7 3.9 fusion.70
  278.0 3.3 bitcast_reduce_fusion.2
  283.9 3.9 fusion.70
  289.2 3.3 bitcast_reduce_fusion.2
  295.1 3.9 fusion.70
  300.4 3.3 bitcast_reduce_fusion.2
  306.3 3.9 fusion.70
  311.6 3.3 bitcast_reduce_fusion.2
  317.5 3.9 fusion.70
  324.5 3.5 convolution_convert_fusion
  328.0 79.4 %reduce-scatter.2.cloned.1.call-done = bf16[64,3072]{1,0:T(8,128)(2,1)} async-done(((bf16[512,3072]{1,0:T(8,128)(2,1)}), bf16[64,3072]{1,0:T(8,128)(2,1)}) %reduce-scatter.2.cloned.1.call-update) | async-done | bytes 393232 | tf_op jit(solution)/shard_map/reduce_scatter | solution.py:123
  (200 shorter events, 103.0 us)
Async XLA Ops:
  6.5 318.0 %copy-start = (bf16[384,3072]{1,0:T(8,128)(2,1)S(1)}, bf16[384,3072]{1,0:T(8,128)(2,1)}, u32[]{:S(2)}) copy-start(bf16[384,3072]{1,0:T(8,128)(2,1)} %param.23) | copy-start | bytes 7077892
  6.5 13.8 %copy-start.1 = (bf16[512,384]{1,0:T(8,128)(2,1)S(1)}, bf16[512,384]{1,0:T(8,128)(2,1)}, u32[]{:S(2)}) copy-start(bf16[512,384]{1,0:T(8,128)(2,1)} %param.13) | copy-start | bytes 1179652
  6.5 136.0 %all-gather.3.cloned.1.call-start = ((), (), s32[]{:S(2)}) async-start(), calls=%async_computation.3 | async-start | bytes 6684672 | tf_op jit(solution)/shard_map/all_gather | solution.py:80
  7.3 135.2 %all-gather.5.cloned.1.call-start = ((), (), s32[]{:S(2)}) async-start(), calls=%async_computation.4 | async-start | bytes 6684672 | tf_op jit(solution)/shard_map/all_gather | solution.py:81
  9.8 96.1 %all-to-all-start = ((bf16[64,8,384]{2,0,1:T(8,128)(2,1)}), bf16[64,8,384]{2,0,1:T(8,128)(2,1)S(1)}, u32[]{:S(2)}, u32[]{:S(2)}) async-start(bf16[64,8,384]{2,0,1:T(8,128)(2,1)} %bitcast.89), calls=%async_computation | async-start | bytes 786432 | tf_op jit(solution)/shard_map/all_to_all | solution.py:91
  102.4 1.6 copy-start.2
  104.0 9.5 %copy-start.3 = (s32[4,2]{0,1:T(2,128)S(1)}, s32[4,2]{0,1:T(2,128)}, u32[]{:S(2)}) copy-start(s32[4,2]{0,1:T(2,128)} %concatenate.4) | copy-start | bytes 100
  105.9 16.2 %all-to-all-start.1 = ((bf16[64,8,384]{2,0,1:T(8,128)(2,1)}), bf16[64,8,384]{2,0,1:T(8,128)(2,1)}, u32[]{:S(2)}, u32[]{:S(2)}) async-start(bf16[64,8,384]{2,0,1:T(8,128)(2,1)} %bitcast.88), calls=%async_computation.1 | async-start | bytes 786432 | tf_op jit(solution)/shard_map/all_to_all | solution.py:92
  113.4 294.0 %reduce-scatter.2.cloned.1.call-start = ((), (), s32[]{:S(2)}) async-start(), calls=%async_computation.5 | async-start | bytes 3538944 | tf_op jit(solution)/shard_map/reduce_scatter | solution.py:123
  121.3 0.6 copy-start.4
  122.0 15.8 %copy-start.5 = (f32[4,3,128]{2,1,0:T(4,128)S(1)}, f32[4,3,128]{2,1,0:T(4,128)}, u32[]{:S(2)}) copy-start(f32[4,3,128]{2,1,0:T(4,128)} %copy-done.4) | copy-start | bytes 18436
Sparse Core Ops, SparseCore 0:
  9.1 49.4 all-gather.2
  60.3 43.5 all-gather.4
  328.1 79.2 reduce-scatter.1
where the time goes:
time: 417 us; the launch traced here: 414 us
  matrix products  124 us (30%)
  waiting for transfers between devices  80.8 us (19%)
  blocking collectives  68.3 us (16%)
  local copies, waits for them, and re-layouts  64 us (15%)
  other arithmetic  45.4 us (11%)
  starting transfers between devices  16.1 us (4%)
  between operations  14.5 us (3%)
    reduce_scatter x1, waiting for transfers between devices, on_device(): lax.psum_scatter(jnp.dot(joined_heads, w_out, preferred_element_type=jnp....  79.4 us
    dot_general x17, matrix products, attend_block(): jnp.einsum('hqk,khd->hqd', weights.astype(jnp.bfloat16), values_split, pr...  63.7 us
    dot_general x17, matrix products, attend_block(): jnp.einsum('qhd,khd->hqk', queries, keys_split, preferred_element_type=jn...  53 us
    reduce_sum x17, other arithmetic, attend_block(): weight_sum = weight_sum * rescale + jnp.sum(weights, axis=-1)  39.4 us
    unnamed x1, blocking collectives  28 us
    dynamic_slice x48, local copies, waits for them, and re-layouts, attend_keys(): running, unused = lax.scan(step, running, (key_blocks, value_blocks))  25.2 us
    all_gather x1, blocking collectives, on_device(): lax.all_gather(text_v, 'seq', axis=0, tiled=True)  21.3 us
    gather x40, local copies, waits for them, and re-layouts  21 us
  transfers between devices with their start and end apart: 5, of which 1 were waited for; matrix products, arithmetic and copies ran while one was open for 12% of the time, Pallas kernels for 0%

commit v1 on v0

v1 whole, which is shorter than its diff:
```python
import functools
import itertools

import jax
import jax.numpy as jnp
from jax import lax
from jax.experimental import pallas as pl
from jax.experimental.pallas import tpu as pltpu
from jax.sharding import PartitionSpec as P

HD = 128
HEADS = 3
GROUP = HEADS * HD
SUB = 256
ROWS = 512
TEXT = 32
SCALE = HD ** (-0.5) * 1.4426950408889634
DEAD = -1e30
AXES = ("seq", "aud")
NT = (((1,), (1,)), ((), ()))
NN = (((1,), (0,)), ((), ()))
F32 = jnp.float32
BF16 = jnp.bfloat16
PARAMS = pltpu.CompilerParams(vmem_limit_bytes=20 * 2**20)
WIDE = pltpu.CompilerParams(vmem_limit_bytes=60 * 2**20)
COST = pl.CostEstimate(flops=1024, bytes_accessed=1024, transcendentals=0)


def lasting(us):
    return pl.CostEstimate(flops=int(us * 1.15e9), bytes_accessed=1024, transcendentals=0)


TIMES = dict(near_mine=2.4, near_other=2.4, mid=8.0, far_other=2.8, far_mine=26.0, side=2.7)
SMEM = pl.BlockSpec(memory_space=pltpu.SMEM)
VMEM = pl.BlockSpec(memory_space=pltpu.VMEM)
HBM = pl.BlockSpec(memory_space=pltpu.HBM)


def pairs(move):
    index = lambda yl, x, c, yh, z: ((yl * 4 + x) * 2 + c) * 8 + yh * 4 + z
    places = itertools.product(range(2), range(4), range(2), range(2), range(4))
    return [(index(*place), index(*move(*place))) for place in places]


X_A = pairs(lambda yl, x, c, yh, z: (yl, (x + 1 - 2 * c) % 4, c, yh, z))
X_B = pairs(lambda yl, x, c, yh, z: (yl, (x - 1 + 2 * c) % 4, c, yh, z))
Z_A = pairs(lambda yl, x, c, yh, z: (yl, x, c, yh, (z + 1 - 2 * c) % 4))
Z_B = pairs(lambda yl, x, c, yh, z: (yl, x, c, yh, (z - 1 + 2 * c) % 4))
Z_2 = pairs(lambda yl, x, c, yh, z: (yl, x, c, yh, (z + 2) % 4))
Y_LO = pairs(lambda yl, x, c, yh, z: (1 - yl, x, c, yh, z))
Y_NEAR = pairs(lambda yl, x, c, yh, z: (1 - yl, x, c, 1 - yh, z))
Y_HI = pairs(lambda yl, x, c, yh, z: (yl, x, c, 1 - yh, z))
CORE = pairs(lambda yl, x, c, yh, z: (yl, x, 1 - c, yh, z))
Y_HI_CORE = pairs(lambda yl, x, c, yh, z: (yl, x, 1 - c, 1 - yh, z))


def send(array, route):
    return lax.ppermute(array, AXES, route)


def after(value, *others):
    return lax.optimization_barrier((value,) + others)[0]


def with_ones(values):
    return jnp.concatenate([values, jnp.ones((values.shape[0], HD), BF16)], axis=1)


def move(sem, *pairs_of_refs):
    copies = [pltpu.make_async_copy(*pair, sem.at[i]) for i, pair in enumerate(pairs_of_refs)]
    for copy in copies:
        copy.start()
    for copy in copies:
        copy.wait()


def stage_body(_, k, v, tk, tv, own, sem):
    left, right = pl.ds(0, GROUP), pl.ds(GROUP, GROUP)
    above, below = pl.ds(0, ROWS), pl.ds(ROWS, TEXT)
    move(
        sem,
        (k, own.at[above, left]),
        (v, own.at[above, right]),
        (tk, own.at[below, left]),
        (tv, own.at[below, right]),
    )


def stage(*parts):
    return pl.pallas_call(
        stage_body,
        out_shape=jax.ShapeDtypeStruct((ROWS + TEXT, 2 * GROUP), BF16),
        in_specs=[SMEM] + [HBM] * 4,
        out_specs=VMEM,
        scratch_shapes=[pltpu.SemaphoreType.DMA((4,))],
        compiler_params=WIDE,
        cost_estimate=COST,
        name="stage",
    )(*parts)


def split_body(here, w, came, own, keep, give):
    width = own.shape[1]
    half = pl.ds(pl.multiple_of(here[0] * width, width), width)
    rest = pl.ds(pl.multiple_of((1 - here[0]) * width, width), width)
    own[...] = w[:, half]
    keep[...] = came[:, half]
    give[...] = came[:, rest]


def split(here, w, came):
    half = jax.ShapeDtypeStruct((w.shape[0], w.shape[1] // 2), BF16)
    return pl.pallas_call(
        split_body,
        out_shape=[half] * 3,
        in_specs=[SMEM, VMEM, VMEM],
        out_specs=[VMEM] * 3,
        compiler_params=PARAMS,
        cost_estimate=COST,
        name="split",
    )(here, w, came)


def lend_body(here, ak, av, out, sem):
    width = out.shape[1]
    rows = ak.shape[0]
    cols = pl.ds(pl.multiple_of((1 - here[3]) * width, width), width)
    move(sem, (ak.at[:, cols], out.at[pl.ds(0, rows)]), (av.at[:, cols], out.at[pl.ds(rows, rows)]))


def lend(here, ak, av):
    return pl.pallas_call(
        lend_body,
        out_shape=jax.ShapeDtypeStruct((2 * ak.shape[0], ak.shape[1] // 2), BF16),
        in_specs=[SMEM, HBM, HBM],
        out_specs=VMEM,
        scratch_shapes=[pltpu.SemaphoreType.DMA((2,))],
        compiler_params=PARAMS,
        cost_estimate=COST,
        name="lend",
    )(here, ak, av)


def prompt_body(*refs):
    for number, ref in enumerate(refs[:-1]):
        refs[-1][pl.ds(number * TEXT, TEXT), :] = ref[...]


BELOW = pl.BlockSpec((TEXT, 2 * GROUP), lambda i: (ROWS // TEXT, 0))


def prompt(*arrays):
    return pl.pallas_call(
        prompt_body,
        out_shape=jax.ShapeDtypeStruct((len(arrays) * TEXT, 2 * GROUP), BF16),
        grid=(1,),
        in_specs=[BELOW] * len(arrays),
        out_specs=VMEM,
        compiler_params=PARAMS,
        cost_estimate=COST,
        name="prompt",
    )(*arrays)


def deal_body(here, ak, av, lent, *outs):
    core, y_hi, z = here[0], here[3], here[4]
    rows = ak.shape[0]
    step = 1 - 2 * core
    for out, shift in zip(outs, (0, step, -step, 2)):
        target = lax.rem(z + shift + 4, 4)
        cols = pl.ds(pl.multiple_of((y_hi * 4 + target) * GROUP, GROUP), GROUP)
        out[:rows, :] = ak[:, cols]
        out[rows : 2 * rows, :] = av[:, cols]
        out[2 * rows :, :] = lent[:, pl.ds(pl.multiple_of(target * GROUP, GROUP), GROUP)]


def deal(here, ak, av, lent):
    return pl.pallas_call(
        deal_body,
        out_shape=[jax.ShapeDtypeStruct((4 * ak.shape[0], GROUP), BF16)] * 4,
        in_specs=[SMEM, VMEM, VMEM, VMEM],
        out_specs=[VMEM] * 4,
        compiler_params=PARAMS,
        cost_estimate=COST,
        name="deal",
    )(here, ak, av, lent)


def digits(column, count):
    out = []
    for _ in range(count):
        digit = column.astype(BF16).astype(F32)
        column = column - digit
        out.append(digit)
    return out


def undigit(table, head, first, count):
    row = lax.broadcasted_iota(jnp.int32, (HD, HD), 0)
    picked = (row % HEADS == head) & (row >= first * HEADS) & (row < (first + count) * HEADS)
    return lax.dot_general(table, picked.astype(F32).astype(BF16), NN, preferred_element_type=F32)


def blend(parts):
    peak = functools.reduce(jnp.maximum, [part[1] for part in parts])
    scales = [jnp.exp2(part[1] - peak) for part in parts]
    mixed = functools.reduce(lambda a, b: a + b, [p[0] * w for p, w in zip(parts, scales)])
    weight = functools.reduce(lambda a, b: a + b, [p[2] * w for p, w in zip(parts, scales)])
    return mixed, peak, weight


def flash_body(n_arrays, n_sets, n_priors, packed, *refs):
    arrays = refs[:n_arrays]
    queries = refs[n_arrays : n_arrays + n_sets]
    refs = refs[n_arrays + n_sets :]
    priors = refs[: 3 * n_sets * n_priors]
    outs = refs[3 * n_sets * n_priors :]
    lane = lax.broadcasted_iota(jnp.int32, (SUB, HD), 1)
    for number in range(n_sets):
        for start in range(0, ROWS, SUB):
            rows = pl.ds(start, SUB)
            table = jnp.zeros((SUB, HD), F32)
            for head in range(HEADS):
                cols = pl.ds(head * HD, HD)
                vcols = pl.ds(GROUP + head * HD, HD)
                q = queries[number][rows, cols]
                scores = []
                peak = None
                for array in arrays:
                    s = lax.dot_general(q, array[:ROWS, cols], NT, preferred_element_type=F32) * SCALE
                    scores.append(s)
                    top = jnp.max(s, axis=1, keepdims=True)
                    peak = top if peak is None else jnp.maximum(peak, top)
                total = None
                for s, array in zip(scores, arrays):
                    p = jnp.exp2(s - peak).astype(BF16)
                    v = with_ones(array[:ROWS, vcols])
                    part = lax.dot_general(p, v, NN, preferred_element_type=F32)
                    total = part if total is None else total + part
                result = (total[:, :HD], jnp.broadcast_to(peak, (SUB, HD)), total[:, HD:])
                if n_priors:
                    parts = [result]
                    for i in range(n_priors):
                        at = 3 * (number * n_priors + i)
                        parts.append(tuple(priors[at + j][rows, cols] for j in range(3)))
                    result = blend(parts)
                if packed:
                    outs[number][rows, cols] = result[0].astype(BF16)
                    for piece, digit in enumerate(digits(result[1], 3) + digits(result[2], 2)):
                        table = jnp.where(lane == piece * HEADS + head, digit, table)
                else:
                    for j in range(3):
                        outs[3 * number + j][rows, cols] = result[j]
            if packed:
                outs[number][rows, GROUP:] = table.astype(BF16)


def flash(name, arrays, queries, priors=None, packed=False):
    n_sets, n_arrays = len(queries), len(arrays)
    priors = priors or [[] for _ in queries]
    n_priors = len(priors[0])
    flat = [ref for parts in priors for part in parts for ref in part]
    if packed:
        shapes = [jax.ShapeDtypeStruct((ROWS, GROUP + HD), BF16)] * n_sets
    else:
        shapes = [jax.ShapeDtypeStruct((ROWS, GROUP), F32)] * (3 * n_sets)
    outs = pl.pallas_call(
        functools.partial(flash_body, n_arrays, n_sets, n_priors, packed),
        out_shape=shapes,
        compiler_params=PARAMS,
        cost_estimate=lasting(TIMES[name]),
        name=name,
    )(*arrays, *queries, *flat)
    return outs if packed else [tuple(outs[3 * i : 3 * i + 3]) for i in range(n_sets)]


def side_body(here, start_ref, length_ref, prompt_ref, q_ref, *refs):
    audios, texts, out_ref = refs[:4], refs[4:14], refs[14]
    core, x, y_lo, y_hi, z = [here[i] for i in range(5)]
    lane = lax.broadcasted_iota(jnp.int32, (1, 16 * TEXT), 1)
    place = jnp.zeros((1, 16 * TEXT), jnp.int32)
    for number in range(16):
        y = y_lo if number < 8 else 1 - y_lo
        c = core if number % 8 < 4 else 1 - core
        step = 2 * c - 1
        shift = (0, step, -step, 2)[number % 4]
        block = y * 8 + lax.rem(x + shift + 4, 4) * 2 + c
        place = jnp.where(lane // TEXT == number, block * TEXT + lane % TEXT, place)
    live = place < prompt_ref[0]
    shard = audios[0].shape[0] // 4
    heard_at = jnp.zeros((1, 8 * shard), jnp.int32)
    lane = lax.broadcasted_iota(jnp.int32, (1, 8 * shard), 1)
    step = 1 - 2 * core
    for number in range(8):
        source = lax.rem(z + (0, -step, step, 2)[number // 2] + 4, 4)
        y = y_hi if number % 2 == 0 else 1 - y_hi
        block = y * 4 + source
        heard_at = jnp.where(lane // shard == number, block * shard + lane % shard, heard_at)
    for head in range(HEADS):
        cols = pl.ds(head * HD, HD)
        vcols = pl.ds(GROUP + head * HD, HD)
        text_k = jnp.concatenate([ref[:, cols] for ref in texts], axis=0)
        text_v = with_ones(jnp.concatenate([ref[:, vcols] for ref in texts], axis=0))
        parts = [(ref, half) for ref in audios for half in (0, 2 * shard)]
        audio_k = jnp.concatenate([ref[pl.ds(half, shard), cols] for ref, half in parts], axis=0)
        audio_v = [ref[pl.ds(half + shard, shard), cols] for ref, half in parts]
        audio_v = with_ones(jnp.concatenate(audio_v, axis=0))
        for block in range(ROWS // HD):
            rows = pl.ds(block * HD, HD)
            q = q_ref[rows, cols]
            s = lax.dot_general(q, text_k, NT, preferred_element_type=F32) * SCALE
            s = jnp.where(live, s, DEAD)
            p = jnp.exp2(s - jnp.max(s, axis=1, keepdims=True)).astype(BF16)
            mix = lax.dot_general(p, text_v, NN, preferred_element_type=F32)
            s = lax.dot_general(q, audio_k, NT, preferred_element_type=F32) * SCALE
            begin = start_ref[block]
            inside = (heard_at >= begin) & (heard_at < begin + length_ref[block])
            s = jnp.where(inside, s, DEAD)
            p = jnp.exp2(s - jnp.max(s, axis=1, keepdims=True)).astype(BF16)
            heard = lax.dot_general(p, audio_v, NN, preferred_element_type=F32)
            out_ref[rows, cols] = heard[:, :HD] / heard[:, HD:] + mix[:, :HD] / mix[:, HD:]


def side(here, block_start, block_len, prompt_len, q, audios, texts, pair_texts):
    return pl.pallas_call(
        side_body,
        out_shape=jax.ShapeDtypeStruct(q.shape, F32),
        grid=(1,),
        in_specs=[SMEM] * 4 + [VMEM] * 5 + [BELOW] * 8 + [VMEM] * 2,
        out_specs=VMEM,
        compiler_params=PARAMS,
        cost_estimate=lasting(TIMES["side"]),
        name="side",
    )(here, block_start, block_len, prompt_len, q, *audios, *texts, *pair_texts)


def join_body(here, *refs):
    mine, packed_ref, side_ref, outs, joined = refs[:3], refs[3], refs[4], refs[5:9], refs[9]
    for head in range(HEADS):
        cols = pl.ds(head * HD, HD)
        table = packed_ref[:, GROUP:]
        other = (
            packed_ref[:, cols].astype(F32),
            undigit(table, head, 0, 3),
            undigit(table, head, 3, 2),
        )
        mixed, _, weight = blend([tuple(ref[:, cols] for ref in mine), other])
        joined[:, cols] = (mixed / weight + side_ref[:, cols]).astype(BF16)
    core, y_hi, z = here[0], here[3], here[4]
    step = 1 - 2 * core
    for out, shift in zip(outs, (0, step, -step, 2)):
        target = lax.rem(z + shift + 4, 4)
        for part in range(2):
            y = y_hi if part == 0 else 1 - y_hi
            start = pl.multiple_of(y * 256 + target * 64, 64)
            out[pl.ds(part * 64, 64), :] = joined[pl.ds(start, 64), :]


def join(here, mine, packed, side_part):
    return pl.pallas_call(
        join_body,
        out_shape=[jax.ShapeDtypeStruct((ROWS // 4, GROUP), BF16)] * 4,
        in_specs=[SMEM] + [VMEM] * 5,
        out_specs=[VMEM] * 4,
        scratch_shapes=[pltpu.VMEM((ROWS, GROUP), BF16)],
        compiler_params=PARAMS,
        cost_estimate=COST,
        name="join",
    )(here, *mine, packed, side_part)


def project_body(*refs):
    here, there, weights = refs[:4], refs[4:8], refs[8:12]
    keep, pair, core, both = refs[12:]
    width = keep.shape[1]
    left = [jnp.concatenate([here[i][...], there[j][...]], axis=0) for i, j in enumerate((0, 2, 1, 3))]
    tile = 512
    for start in range(0, width, tile):
        cols = pl.ds(start, tile)
        total = None
        for rows, w in zip(left, weights):
            part = lax.dot_general(rows, w[:, cols], NN, preferred_element_type=F32)
            total = part if total is None else total + part
        keep[:, cols] = total[:64]
        pair[:, cols] = total[64:128].astype(BF16)
        core[:, cols] = total[128:192].astype(BF16)
        both[:, cols] = total[192:].astype(BF16)


def project(here, there, weights):
    width = weights[0].shape[1]
    shape = lambda dtype: jax.ShapeDtypeStruct((64, width), dtype)
    return pl.pallas_call(
        project_body,
        out_shape=[shape(F32), shape(BF16), shape(BF16), shape(BF16)],
        compiler_params=PARAMS,
        cost_estimate=COST,
        name="project",
    )(*here, *there, *weights)


def total_body(here, keep, pair, core, both, out):
    width = keep.shape[1]
    mine = (keep[...] + pair[...].astype(F32)).astype(BF16)
    other = (core[...].astype(F32) + both[...].astype(F32)).astype(BF16)

    @pl.when(here[0] == 0)
    def _():
        out[:, :width] = mine
        out[:, width:] = other

    @pl.when(here[0] != 0)
    def _():
        out[:, :width] = other
        out[:, width:] = mine


def total(here, keep, pair, core, both):
    return pl.pallas_call(
        total_body,
        out_shape=jax.ShapeDtypeStruct((keep.shape[0], 2 * keep.shape[1]), BF16),
        in_specs=[SMEM] + [VMEM] * 4,
        out_specs=VMEM,
        compiler_params=PARAMS,
        cost_estimate=COST,
        name="total",
    )(here, keep, pair, core, both)


def on_device(
    video_q,
    video_k,
    video_v,
    audio_k,
    audio_v,
    text_k,
    text_v,
    block_start,
    block_len,
    prompt_len,
    w_out,
):
    seq = lax.axis_index("seq")
    aud = lax.axis_index("aud")
    here = jnp.stack([seq % 2, (seq // 2) % 4, seq // 8, aud // 4, aud % 4]).astype(jnp.int32)

    own = stage(here, video_k, video_v, text_k, text_v)
    own_c = send(own, CORE)
    kv1 = send(own, X_A)
    kv2 = send(own, X_B)
    asked = send(video_q, Y_LO)
    lent = send(lend(here, audio_k, audio_v), Y_NEAR)
    came = send(w_out, Z_A)
    (near_mine,) = flash("near_mine", [own, own_c], [video_q])
    (near_other,) = flash("near_other", [own, own_c], [asked])
    kv1, kv2, near_mine, near_other, lent = lax.optimization_barrier(
        (kv1, kv2, near_mine, near_other, lent)
    )
    dealt = deal(here, audio_k, audio_v, lent)
    audios = [dealt[0], send(dealt[1], Z_A), send(dealt[2], Z_B), send(dealt[3], Z_2)]
    kv3 = send(kv1, X_A)
    kv1_c = send(kv1, CORE)
    kv2_c = send(kv2, CORE)
    mid_mine, mid_other = flash("mid", [kv1, kv2, kv1_c, kv2_c], [after(video_q, came), asked])
    kv3, mid_mine, mid_other, *audios = lax.optimization_barrier(
        (kv3, mid_mine, mid_other, *audios)
    )
    kv3_c = send(kv3, CORE)
    text = prompt(own, kv1, kv2, kv3)
    text_y = send(text, Y_LO)
    (packed,) = flash(
        "far_other", [kv3, kv3_c], [asked], [[near_other, mid_other]], packed=True
    )
    packed, text_y = lax.optimization_barrier((packed, text_y))
    got = send(packed, Y_LO)
    w0, w1, w2 = split(here, w_out, after(came, packed))
    w3 = send(w1, Z_A)
    w2 = send(w2, CORE)
    text_yc = send(text_y, CORE)
    (far_mine,) = flash("far_mine", [kv3, kv3_c], [after(video_q, packed, w2)], [[near_mine, mid_mine]])
    side_part = side(
        here,
        block_start,
        block_len,
        prompt_len,
        after(video_q, packed),
        audios,
        [own, kv1, kv2, kv3, own_c, kv1_c, kv2_c, kv3_c],
        [text_y, text_yc],
    )

    parts = join(here, far_mine, got, side_part)
    mine = [parts[0], send(parts[1], Z_A), send(parts[2], Z_B), send(parts[3], Z_2)]
    theirs = [send(part, CORE) for part in mine]
    keep, pair, cross, both = project(mine, theirs, [w0, w1, w2, w3])
    pair = send(pair, Y_HI)
    both = send(both, Y_HI_CORE)
    cross = send(cross, CORE)
    return total(here, keep, pair, cross, both)


def solution(mesh):
    placed = (
        P("seq", "aud"),
        P("seq", "aud"),
        P("seq", "aud"),
        P("aud", None),
        P("aud", None),
        P("seq", "aud"),
        P("seq", "aud"),
        P("seq"),
        P("seq"),
        P(),
        P("aud", None),
    )
    return jax.shard_map(
        on_device, mesh=mesh, in_specs=placed, out_specs=P(("seq", "aud"), None), check_vma=False
    )
```

time: 417 us -> 97 us (0.23)
  matrix products: 124 us -> 0 us
  blocking collectives: 68.3 us -> 0 us
  local copies, waits for them, and re-layouts: 64 us -> 0.63 us
  waiting for transfers between devices: 80.8 us -> 28.1 us
  other arithmetic: 45.4 us -> 0 us
  Pallas kernels: 0 us -> 31.1 us
  starting transfers between devices: 16.1 us -> 36.1 us
  between operations: 14.5 us -> 0.89 us
    dot_general x37 -> x0, matrix products: 124 us -> none  [the longest x17 63.7 us: attend_block(): jnp.einsum('hqk,khd->hqd', weights.astype(jnp.bfloat16), values_split, pr...]
    reduce_scatter x1 -> x0, waiting for transfers between devices: 79.4 us -> none  [on_device(): lax.psum_scatter(jnp.dot(joined_heads, w_out, preferred_element_type=jnp....]
    all_gather x2 -> x0, blocking collectives: 40.3 us -> none  [the longest x1 21.3 us: on_device(): lax.all_gather(text_v, 'seq', axis=0, tiled=True)]
    reduce_sum x18 -> x0, other arithmetic: 39.5 us -> none  [the longest x17 39.4 us: attend_block(): weight_sum = weight_sum * rescale + jnp.sum(weights, axis=-1)]
    ppermute x0 -> x28, starting transfers between devices: none -> 36.1 us  [send(): return lax.ppermute(array, AXES, route)]
    pallas_call x0 -> x14, Pallas kernels: none -> 31.1 us  [the longest x5 19.1 us: flash(): pl.pallas_call(functools.partial(flash_body, n_arrays, n_sets, n_priors,...]
    ppermute x0 -> x28, waiting for transfers between devices: none -> 28.1 us  [send(): return lax.ppermute(array, AXES, route)]
    unnamed x1 -> x0, blocking collectives: 28 us -> none
  transfers between devices with their start and end apart: 5 -> 28, of which waited for: 1 -> 10; matrix products, arithmetic and copies ran while one was open for 12% -> 1% of each run, Pallas kernels for 0% -> 28%
where the time goes in v1:
time: 97 us; the launch traced here: 96.9 us
  starting transfers between devices  36.1 us (37%)
  Pallas kernels  31.1 us (32%)
  waiting for transfers between devices  28.1 us (29%)
    ppermute x28, starting transfers between devices, send(): return lax.ppermute(array, AXES, route)  36.1 us
    ppermute x28, waiting for transfers between devices, send(): return lax.ppermute(array, AXES, route)  28.1 us
    pallas_call x5, Pallas kernels, flash(): pl.pallas_call(functools.partial(flash_body, n_arrays, n_sets, n_priors,...  19.1 us
    pallas_call x1, Pallas kernels, stage(): pl.pallas_call(stage_body, out_shape=jax.ShapeDtypeStruct((ROWS + TEXT, 2...  2.85 us
    pallas_call x1, Pallas kernels, side(): pl.pallas_call(side_body, out_shape=jax.ShapeDtypeStruct(q.shape, F32), g...  2.73 us
  transfers between devices with their start and end apart: 28, of which 10 were waited for; matrix products, arithmetic and copies ran while one was open for 1% of the time, Pallas kernels for 28%

profile of v1, /device:TPU:1, one launch (start us, length us, event | category | flops | bytes accessed | tf_op | source)
XLA Modules:
  0.0 96.9 jit_solution(5283180585246470859)
XLA Ops:
  0.0 4.7 %collective-permute-start.8 = (bf16[384,3072]{1,0:T(8,128)(2,1)}, bf16[384,3072]{1,0:T(8,128)(2,1)S(1)}, u32[]{:S(2)}, u32[]{:S(2)}) collective-permute-start(bf16[384,3072]{1,0:T(8,128)(2,1)} %w.1), channel_id=1, source_target_pairs={{0,1},{1,2},{2,3},{3,0},{4,5},{5,6},{6,7},{7,4},{8,11},{9,8},{10,9... | collective-permute-start | bytes 7077896 | tf_op jit(solution)/shard_map/ppermute | solution.py:58
  4.7 0.6 stack.23._.here
  5.3 2.9 %stage.1.refs_0_.refs_4_ = bf16[544,768]{1,0:T(8,128)(2,1)} custom-call(s32[5]{0:T(128)} %stack.23._.here, bf16[512,384]{1,0:T(8,128)(2,1)} %k.1, bf16[512,384]{1,0:T(8,128)(2,1)} %v.1, bf16[32,384]{1,0:T(8,128)(2,1)} %tk.1, bf16[32,384]{1,0:T(8,128)(2,1)} %tv.1), custom_call_target="tpu_custom_call" | custom-call | flops 1024 | bytes 1024 | tf_op jit(solution)/shard_map/stage/pallas_call | solution.py:90
  8.1 0.1 collective-permute-start.2
  8.2 2.5 %collective-permute-start = (bf16[544,768]{1,0:T(8,128)(2,1)}, bf16[544,768]{1,0:T(8,128)(2,1)S(1)}, u32[]{:S(2)}, u32[]{:S(2)}) collective-permute-start(bf16[544,768]{1,0:T(8,128)(2,1)} %stage.1.refs_0_.refs_4_), channel_id=1, source_target_pairs={{0,16},{1,17},{2,18},{3,19},{4,20},{5,21},{6,22},{7,23},{8,56},{9,... | collective-permute-start | bytes 2506760 | tf_op jit(solution)/shard_map/ppermute | solution.py:58
  10.8 1.3 %collective-permute-start.3 = (bf16[512,384]{1,0:T(8,128)(2,1)S(1)}, bf16[512,384]{1,0:T(8,128)(2,1)S(1)}, u32[]{:S(2)}, u32[]{:S(2)}) collective-permute-start(bf16[512,384]{1,0:T(8,128)(2,1)S(1)} %copy-done.5), channel_id=1, source_target_pairs={{0,64},{1,65},{2,66},{3,67},{4,68},{5,69},{6,70},{7,71},{8,72},{9,... | collective-permute-start | bytes 1179656 | tf_op jit(solution)/shard_map/ppermute | solution.py:58
  12.1 0.6 lend.1
  12.7 2.0 %collective-permute-start.4 = (bf16[128,1536]{1,0:T(8,128)(2,1)S(1)}, bf16[128,1536]{1,0:T(8,128)(2,1)S(1)}, u32[]{:S(2)}, u32[]{:S(2)}) collective-permute-start(bf16[128,1536]{1,0:T(8,128)(2,1)S(1)} %lend.1), channel_id=1, source_target_pairs={{0,68},{1,69},{2,70},{3,71},{4,64},{5,65},{6,66},{7,67},{8,76},{9,... | collective-permute-start | bytes 1179656 | tf_op jit(solution)/shard_map/ppermute | solution.py:58
  14.7 2.4 %near_mine.1 = (f32[512,384]{1,0:T(8,128)S(1)}, f32[512,384]{1,0:T(8,128)S(1)}, f32[512,384]{1,0:T(8,128)S(1)}) custom-call(bf16[544,768]{1,0:T(8,128)(2,1)S(1)} %copy-done, bf16[544,768]{1,0:T(8,128)(2,1)S(1)} %collective-permute-done.2.refs_1_.refs_8_, bf16[512,384]{1,0:T(8,128)(2,1)S(1)} %copy-done.5), custom_call_target="tpu_custom_call" | custom-call | flops 2760000000 | bytes 1024 | tf_op jit(solution)/shard_map/near_mine/pallas_call | solution.py:267
  17.2 3.0 %collective-permute-done.3.refs_2_.refs_5_ = bf16[512,384]{1,0:T(8,128)(2,1)S(1)} collective-permute-done((bf16[512,384]{1,0:T(8,128)(2,1)S(1)}, bf16[512,384]{1,0:T(8,128)(2,1)S(1)}, u32[]{:S(2)}, u32[]{:S(2)}) %collective-permute-start.3) | collective-permute-done | bytes 393248 | tf_op jit(solution)/shard_map/ppermute | solution.py:58
  20.2 2.4 %near_other.1 = (f32[512,384]{1,0:T(8,128)S(1)}, f32[512,384]{1,0:T(8,128)S(1)}, f32[512,384]{1,0:T(8,128)S(1)}) custom-call(bf16[544,768]{1,0:T(8,128)(2,1)S(1)} %copy-done, bf16[544,768]{1,0:T(8,128)(2,1)S(1)} %collective-permute-done.2.refs_1_.refs_8_, bf16[512,384]{1,0:T(8,128)(2,1)S(1)} %collective-permute-done.3.refs_2_.refs_5_), custom_call_target="tpu_custom_call" | custom-call | flops 2760000000 | bytes 1024 | tf_op jit(solution)/shard_map/near_other/pallas_call | solution.py:267
  22.6 0.5 collective-permute-done.4.lent
  23.2 4.9 %collective-permute-done.refs_0_.refs_1_.refs_5_ = bf16[544,768]{1,0:T(8,128)(2,1)S(1)} collective-permute-done((bf16[544,768]{1,0:T(8,128)(2,1)}, bf16[544,768]{1,0:T(8,128)(2,1)S(1)}, u32[]{:S(2)}, u32[]{:S(2)}) %collective-permute-start) | collective-permute-done | bytes 835616 | tf_op jit(solution)/shard_map/ppermute | solution.py:58
  28.1 3.1 %collective-permute-done.1.refs_1_.refs_2_.refs_6_ = bf16[544,768]{1,0:T(8,128)(2,1)S(1)} collective-permute-done((bf16[544,768]{1,0:T(8,128)(2,1)}, bf16[544,768]{1,0:T(8,128)(2,1)S(1)}, u32[]{:S(2)}, u32[]{:S(2)}) %collective-permute-start.1) | collective-permute-done | bytes 835616 | tf_op jit(solution)/shard_map/ppermute | solution.py:58
  31.2 0.5 collective-permute-start.7
  31.7 1.5 %collective-permute-start.5 = (bf16[544,768]{1,0:T(8,128)(2,1)S(1)}, bf16[544,768]{1,0:T(8,128)(2,1)S(1)}, u32[]{:S(2)}, u32[]{:S(2)}) collective-permute-start(bf16[544,768]{1,0:T(8,128)(2,1)S(1)} %collective-permute-done.refs_0_.refs_1_.refs_5_), channel_id=1, source_target_pairs={{0,16},{1,17},{2,18},{3,19},{4,20},{5,21},{6,22},{7,23},{8,56},{9,... | collective-permute-start | bytes 2506760 | tf_op jit(solution)/shard_map/ppermute | solution.py:58
  33.2 0.6 deal.1
  33.8 0.7 collective-permute-start.9
  34.6 0.8 collective-permute-start.10
  35.4 2.1 %collective-permute-start.11 = (bf16[256,384]{1,0:T(8,128)(2,1)S(1)}, bf16[256,384]{1,0:T(8,128)(2,1)S(1)}, u32[]{:S(2)}, u32[]{:S(2)}) collective-permute-start(bf16[256,384]{1,0:T(8,128)(2,1)S(1)} %get-tuple-element.80), channel_id=1, source_target_pairs={{0,2},{1,3},{2,0},{3,1},{4,6},{5,7},{6,4},{7,5},{8,10},{9,11},{10,... | collective-permute-start | bytes 589832 | tf_op jit(solution)/shard_map/ppermute | solution.py:58
  37.4 8.4 %mid.1 = (f32[512,384]{1,0:T(8,128)S(1)}, f32[512,384]{1,0:T(8,128)S(1)}, f32[512,384]{1,0:T(8,128)S(1)}, f32[512,384]{1,0:T(8,128)S(1)}, f32[512,384]{1,0:T(8,128)S(1)}, /*index=5*/f32[512,384]{1,0:T(8,128)S(1)}) custom-call(bf16[544,768]{1,0:T(8,128)(2,1)S(1)} %collective-permute-done.refs_0_.refs_1_.refs_5_, ...), custom_call_target="tpu_custom_call" | custom-call | flops 9200000000 | bytes 1024 | tf_op jit(solution)/shard_map/mid/pallas_call | solution.py:267
  45.9 0.1 collective-permute-start.12
  46.0 1.4 %collective-permute-start.13 = (bf16[128,768]{1,0:T(8,128)(2,1)S(1)}, bf16[128,768]{1,0:T(8,128)(2,1)S(1)}, u32[]{:S(2)}, u32[]{:S(2)}) collective-permute-start(bf16[128,768]{1,0:T(8,128)(2,1)S(1)} %prompt.1), channel_id=1, source_target_pairs={{0,64},{1,65},{2,66},{3,67},{4,68},{5,69},{6,70},{7,71},{8,72},{9,... | collective-permute-start | bytes 589832 | tf_op jit(solution)/shard_map/ppermute | solution.py:58
  47.4 0.9 collective-permute-done.12.refs_1_.refs_11_
  48.3 3.0 %far_other.1 = bf16[512,512]{1,0:T(8,128)(2,1)S(1)} custom-call(bf16[544,768]{1,0:T(8,128)(2,1)S(1)} %collective-permute-done.5.refs_0_.refs_3_.refs_7_, bf16[544,768]{1,0:T(8,128)(2,1)S(1)} %collective-permute-done.12.refs_1_.refs_11_, bf16[512,384]{1,0:T(8,128)(2,1)S(1)} %collective-permute-done.3.refs_2_.refs_5_, ...), custom_call_target="tpu_custom_call" | custom-call | flops 3220000000 | bytes 1024 | tf_op jit(solution)/shard_map/far_other/pallas_call | solution.py:267
  51.3 0.7 collective-permute-done.13.refs_12_
  52.1 0.8 split.1
  52.9 1.6 %collective-permute-start.14 = (bf16[384,1536]{1,0:T(8,128)(2,1)S(1)}, bf16[384,1536]{1,0:T(8,128)(2,1)S(1)}, u32[]{:S(2)}, u32[]{:S(2)}) collective-permute-start(bf16[384,1536]{1,0:T(8,128)(2,1)S(1)} %get-tuple-element.90), channel_id=1, source_target_pairs={{0,8},{1,9},{2,10},{3,11},{4,12},{5,13},{6,14},{7,15},{8,0},{9,1},... | collective-permute-start | bytes 3538952 | tf_op jit(solution)/shard_map/ppermute | solution.py:58
  54.5 0.1 collective-permute-start.16
  55.3 1.4 %collective-permute-start.15 = (bf16[512,512]{1,0:T(8,128)(2,1)S(1)}, bf16[512,512]{1,0:T(8,128)(2,1)S(1)}, u32[]{:S(2)}, u32[]{:S(2)}) collective-permute-start(bf16[512,512]{1,0:T(8,128)(2,1)S(1)} %far_other.1), channel_id=1, source_target_pairs={{0,64},{1,65},{2,66},{3,67},{4,68},{5,69},{6,70},{7,71},{8,72},{9,... | collective-permute-start | bytes 1572872 | tf_op jit(solution)/shard_map/ppermute | solution.py:58
  56.6 1.1 %collective-permute-start.24 = (bf16[384,1536]{1,0:T(8,128)(2,1)S(1)}, bf16[384,1536]{1,0:T(8,128)(2,1)S(1)}, u32[]{:S(2)}, u32[]{:S(2)}) collective-permute-start(bf16[384,1536]{1,0:T(8,128)(2,1)S(1)} %get-tuple-element.112.refs_9_), channel_id=1, source_target_pairs={{0,1},{1,2},{2,3},{3,0},{4,5},{5,6},{6,7},{7,4},{8,11},{9,8},{10,9... | collective-permute-start | bytes 3538952 | tf_op jit(solution)/shard_map/ppermute | solution.py:58
  57.7 2.7 %side.1.refs_4_ = f32[512,384]{1,0:T(8,128)S(1)} custom-call(s32[5]{0:T(128)S(1)} %copy-done.4, s32[4]{0:T(128)S(1)} %copy-done.6, s32[4]{0:T(128)S(1)} %copy-done.7, s32[1]{0:T(128)S(6)} %copy.12.prompt_ref, bf16[512,384]{1,0:T(8,128)(2,1)S(1)} %copy-done.5, bf16[256,384]{1,0:T(8,128)(2,1)S(1)} %get-tuple-element.102.refs_0_, ...), custom_call_target="tpu_custom_call" | custom-call | flops 3104999936 | bytes 1024 | tf_op jit(solution)/shard_map/side/pallas_call | solution.py:325
  60.5 2.8 %far_mine.1 = (f32[512,384]{1,0:T(8,128)S(1)}, f32[512,384]{1,0:T(8,128)S(1)}, f32[512,384]{1,0:T(8,128)S(1)}) custom-call(bf16[544,768]{1,0:T(8,128)(2,1)S(1)} %collective-permute-done.5.refs_0_.refs_3_.refs_7_, bf16[544,768]{1,0:T(8,128)(2,1)S(1)} %collective-permute-done.12.refs_1_.refs_11_, bf16[512,384]{1,0:T(8,128)(2,1)S(1)} %copy-done.5, ...), custom_call_target="tpu_custom_call" | custom-call | flops 29899999232 | bytes 1024 | tf_op jit(solution)/shard_map/far_mine/pallas_call | solution.py:267
  63.3 5.1 %collective-permute-done.15.refs_3_ = bf16[512,512]{1,0:T(8,128)(2,1)S(1)} collective-permute-done((bf16[512,512]{1,0:T(8,128)(2,1)S(1)}, bf16[512,512]{1,0:T(8,128)(2,1)S(1)}, u32[]{:S(2)}, u32[]{:S(2)}) %collective-permute-start.15) | collective-permute-done | bytes 524320 | tf_op jit(solution)/shard_map/ppermute | solution.py:58
  68.4 1.2 %join.1 = (bf16[128,384]{1,0:T(8,128)(2,1)S(1)}, bf16[128,384]{1,0:T(8,128)(2,1)S(1)}, bf16[128,384]{1,0:T(8,128)(2,1)S(1)}, bf16[128,384]{1,0:T(8,128)(2,1)S(1)}) custom-call(s32[5]{0:T(128)S(1)} %copy-done.4, f32[512,384]{1,0:T(8,128)S(1)} %get-tuple-element.98.refs_0_, f32[512,384]{1,0:T(8,128)S(1)} %get-tuple-element.99.refs_1_, ...), custom_call_target="tpu_custom_call" | custom-call | flops 1024 | bytes 1024 | tf_op jit(solution)/shard_map/join/pallas_call | solution.py:360
  69.6 1.2 %collective-permute-start.17 = (bf16[128,384]{1,0:T(8,128)(2,1)S(1)}, bf16[128,384]{1,0:T(8,128)(2,1)S(1)}, u32[]{:S(2)}, u32[]{:S(2)}) collective-permute-start(bf16[128,384]{1,0:T(8,128)(2,1)S(1)} %get-tuple-element.108), channel_id=1, source_target_pairs={{0,1},{1,2},{2,3},{3,0},{4,5},{5,6},{6,7},{7,4},{8,11},{9,8},{10,9... | collective-permute-start | bytes 294920 | tf_op jit(solution)/shard_map/ppermute | solution.py:58
  70.8 0.4 collective-permute-start.18
  71.1 1.8 %collective-permute-start.19 = (bf16[128,384]{1,0:T(8,128)(2,1)S(1)}, bf16[128,384]{1,0:T(8,128)(2,1)S(1)}, u32[]{:S(2)}, u32[]{:S(2)}) collective-permute-start(bf16[128,384]{1,0:T(8,128)(2,1)S(1)} %get-tuple-element.110), channel_id=1, source_target_pairs={{0,2},{1,3},{2,0},{3,1},{4,6},{5,7},{6,4},{7,5},{8,10},{9,11},{10,... | collective-permute-start | bytes 294920 | tf_op jit(solution)/shard_map/ppermute | solution.py:58
  73.0 2.1 %collective-permute-start.20 = (bf16[128,384]{1,0:T(8,128)(2,1)S(1)}, bf16[128,384]{1,0:T(8,128)(2,1)S(1)}, u32[]{:S(2)}, u32[]{:S(2)}) collective-permute-start(bf16[128,384]{1,0:T(8,128)(2,1)S(1)} %get-tuple-element.107.refs_0_), channel_id=1, source_target_pairs={{0,8},{1,9},{2,10},{3,11},{4,12},{5,13},{6,14},{7,15},{8,0},{9,1},... | collective-permute-start | bytes 294920 | tf_op jit(solution)/shard_map/ppermute | solution.py:58
  75.0 3.2 %collective-permute-start.21 = (bf16[128,384]{1,0:T(8,128)(2,1)S(1)}, bf16[128,384]{1,0:T(8,128)(2,1)S(1)}, u32[]{:S(2)}, u32[]{:S(2)}) collective-permute-start(bf16[128,384]{1,0:T(8,128)(2,1)S(1)} %collective-permute-done.17.refs_1_), channel_id=1, source_target_pairs={{0,8},{1,9},{2,10},{3,11},{4,12},{5,13},{6,14},{7,15},{8,0},{9,1},... | collective-permute-start | bytes 294920 | tf_op jit(solution)/shard_map/ppermute | solution.py:58
  78.3 2.0 %collective-permute-start.23 = (bf16[128,384]{1,0:T(8,128)(2,1)S(1)}, bf16[128,384]{1,0:T(8,128)(2,1)S(1)}, u32[]{:S(2)}, u32[]{:S(2)}) collective-permute-start(bf16[128,384]{1,0:T(8,128)(2,1)S(1)} %collective-permute-done.19.refs_3_), channel_id=1, source_target_pairs={{0,8},{1,9},{2,10},{3,11},{4,12},{5,13},{6,14},{7,15},{8,0},{9,1},... | collective-permute-start | bytes 294920 | tf_op jit(solution)/shard_map/ppermute | solution.py:58
  80.3 0.9 collective-permute-done.23.refs_7_
  81.2 1.8 %project.1 = (f32[64,1536]{1,0:T(8,128)S(1)}, bf16[64,1536]{1,0:T(8,128)(2,1)S(1)}, bf16[64,1536]{1,0:T(8,128)(2,1)S(1)}, bf16[64,1536]{1,0:T(8,128)(2,1)S(1)}) custom-call(bf16[128,384]{1,0:T(8,128)(2,1)S(1)} %get-tuple-element.107.refs_0_, bf16[128,384]{1,0:T(8,128)(2,1)S(1)} %collective-permute-done.17.refs_1_, ...), custom_call_target="tpu_custom_call" | custom-call | flops 1024 | bytes 1024 | tf_op jit(solution)/shard_map/project/pallas_call | solution.py:393
  83.0 3.0 %collective-permute-start.25 = (bf16[64,1536]{1,0:T(8,128)(2,1)S(1)}, bf16[64,1536]{1,0:T(8,128)(2,1)S(1)}, u32[]{:S(2)}, u32[]{:S(2)}) collective-permute-start(bf16[64,1536]{1,0:T(8,128)(2,1)S(1)} %get-tuple-element.114), channel_id=1, source_target_pairs={{0,4},{1,5},{2,6},{3,7},{4,0},{5,1},{6,2},{7,3},{8,12},{9,13},{10,... | collective-permute-start | bytes 589832 | tf_op jit(solution)/shard_map/ppermute | solution.py:58
  86.0 0.6 collective-permute-start.26
  86.7 4.1 %collective-permute-done.25.pair = bf16[64,1536]{1,0:T(8,128)(2,1)S(1)} collective-permute-done((bf16[64,1536]{1,0:T(8,128)(2,1)S(1)}, bf16[64,1536]{1,0:T(8,128)(2,1)S(1)}, u32[]{:S(2)}, u32[]{:S(2)}) %collective-permute-start.25) | collective-permute-done | bytes 196640 | tf_op jit(solution)/shard_map/ppermute | solution.py:58
  90.8 4.7 %collective-permute-done.27.both = bf16[64,1536]{1,0:T(8,128)(2,1)S(1)} collective-permute-done((bf16[64,1536]{1,0:T(8,128)(2,1)S(1)}, bf16[64,1536]{1,0:T(8,128)(2,1)S(1)}, u32[]{:S(2)}, u32[]{:S(2)}) %collective-permute-start.27) | collective-permute-done | bytes 196640 | tf_op jit(solution)/shard_map/ppermute | solution.py:58
  95.5 1.4 %total.1 = bf16[64,3072]{1,0:T(8,128)(2,1)} custom-call(s32[5]{0:T(128)S(1)} %copy-done.4, f32[64,1536]{1,0:T(8,128)S(1)} %get-tuple-element.113.keep, bf16[64,1536]{1,0:T(8,128)(2,1)S(1)} %collective-permute-done.25.pair, bf16[64,1536]{1,0:T(8,128)(2,1)S(1)} %collective-permute-done.26.core, bf16[64,1536]{1,0:T(8,128)(2,1)S(1)} %collective-permute-done.27.both), custom_call_target="tpu_custom_call" | custom-call | flops 1024 | bytes 1024 | tf_op jit(solution)/shard_map/total/pallas_call | solution.py:419
  (39 shorter events, 0.1 us)
Async XLA Ops:
  0.0 10.8 %copy-start.5 = (bf16[512,384]{1,0:T(8,128)(2,1)S(1)}, bf16[512,384]{1,0:T(8,128)(2,1)}, u32[]{:S(2)}) copy-start(bf16[512,384]{1,0:T(8,128)(2,1)} %q_ref) | copy-start | bytes 1179652
  0.0 12.1 %copy-start.2 = (bf16[64,3072]{1,0:T(8,128)(2,1)S(1)}, bf16[64,3072]{1,0:T(8,128)(2,1)}, u32[]{:S(2)}) copy-start(bf16[64,3072]{1,0:T(8,128)(2,1)} %ak.3) | copy-start | bytes 1179652
  0.0 12.1 %copy-start.3 = (bf16[64,3072]{1,0:T(8,128)(2,1)S(1)}, bf16[64,3072]{1,0:T(8,128)(2,1)}, u32[]{:S(2)}) copy-start(bf16[64,3072]{1,0:T(8,128)(2,1)} %av.3) | copy-start | bytes 1179652
  0.0 34.6 %collective-permute-start.8 = (bf16[384,3072]{1,0:T(8,128)(2,1)}, bf16[384,3072]{1,0:T(8,128)(2,1)S(1)}, u32[]{:S(2)}, u32[]{:S(2)}) collective-permute-start(bf16[384,3072]{1,0:T(8,128)(2,1)} %w.1), channel_id=1, source_target_pairs={{0,1},{1,2},{2,3},{3,0},{4,5},{5,6},{6,7},{7,4},{8,11},{9,8},{10,9... | collective-permute-start | bytes 7077896 | tf_op jit(solution)/shard_map/ppermute | solution.py:58
  5.3 6.8 %copy-start.4 = (s32[5]{0:T(128)S(1)}, s32[5]{0:T(128)}, u32[]{:S(2)}) copy-start(s32[5]{0:T(128)} %stack.23._.here) | copy-start | bytes 64
  8.1 6.6 %copy-start = (bf16[544,768]{1,0:T(8,128)(2,1)S(1)}, bf16[544,768]{1,0:T(8,128)(2,1)}, u32[]{:S(2)}) copy-start(bf16[544,768]{1,0:T(8,128)(2,1)} %stage.1.refs_0_.refs_4_) | copy-start | bytes 2506756
  8.1 4.6 %collective-permute-start.2 = (bf16[544,768]{1,0:T(8,128)(2,1)}, bf16[544,768]{1,0:T(8,128)(2,1)S(1)}, u32[]{:S(2)}, u32[]{:S(2)}) collective-permute-start(bf16[544,768]{1,0:T(8,128)(2,1)} %stage.1.refs_0_.refs_4_), channel_id=1, source_target_pairs={{0,8},{1,9},{2,10},{3,11},{4,12},{5,13},{6,14},{7,15},{8,0},{9,1},... | collective-permute-start | bytes 2506760 | tf_op jit(solution)/shard_map/ppermute | solution.py:58
  8.2 19.9 %collective-permute-start = (bf16[544,768]{1,0:T(8,128)(2,1)}, bf16[544,768]{1,0:T(8,128)(2,1)S(1)}, u32[]{:S(2)}, u32[]{:S(2)}) collective-permute-start(bf16[544,768]{1,0:T(8,128)(2,1)} %stage.1.refs_0_.refs_4_), channel_id=1, source_target_pairs={{0,16},{1,17},{2,18},{3,19},{4,20},{5,21},{6,22},{7,23},{8,56},{9,... | collective-permute-start | bytes 2506760 | tf_op jit(solution)/shard_map/ppermute | solution.py:58
  10.8 20.4 %collective-permute-start.1 = (bf16[544,768]{1,0:T(8,128)(2,1)}, bf16[544,768]{1,0:T(8,128)(2,1)S(1)}, u32[]{:S(2)}, u32[]{:S(2)}) collective-permute-start(bf16[544,768]{1,0:T(8,128)(2,1)} %stage.1.refs_0_.refs_4_), channel_id=1, source_target_pairs={{0,48},{1,49},{2,50},{3,51},{4,52},{5,53},{6,54},{7,55},{8,24},{9,... | collective-permute-start | bytes 2506760 | tf_op jit(solution)/shard_map/ppermute | solution.py:58
  10.8 9.4 %collective-permute-start.3 = (bf16[512,384]{1,0:T(8,128)(2,1)S(1)}, bf16[512,384]{1,0:T(8,128)(2,1)S(1)}, u32[]{:S(2)}, u32[]{:S(2)}) collective-permute-start(bf16[512,384]{1,0:T(8,128)(2,1)S(1)} %copy-done.5), channel_id=1, source_target_pairs={{0,64},{1,65},{2,66},{3,67},{4,68},{5,69},{6,70},{7,71},{8,72},{9,... | collective-permute-start | bytes 1179656 | tf_op jit(solution)/shard_map/ppermute | solution.py:58
  12.7 10.4 %collective-permute-start.4 = (bf16[128,1536]{1,0:T(8,128)(2,1)S(1)}, bf16[128,1536]{1,0:T(8,128)(2,1)S(1)}, u32[]{:S(2)}, u32[]{:S(2)}) collective-permute-start(bf16[128,1536]{1,0:T(8,128)(2,1)S(1)} %lend.1), channel_id=1, source_target_pairs={{0,68},{1,69},{2,70},{3,71},{4,64},{5,65},{6,66},{7,67},{8,76},{9,... | collective-permute-start | bytes 1179656 | tf_op jit(solution)/shard_map/ppermute | solution.py:58
  31.2 4.2 %collective-permute-start.6 = (bf16[544,768]{1,0:T(8,128)(2,1)S(1)}, bf16[544,768]{1,0:T(8,128)(2,1)S(1)}, u32[]{:S(2)}, u32[]{:S(2)}) collective-permute-start(bf16[544,768]{1,0:T(8,128)(2,1)S(1)} %collective-permute-done.refs_0_.refs_1_.refs_5_), channel_id=1, source_target_pairs={{0,8},{1,9},{2,10},{3,11},{4,12},{5,13},{6,14},{7,15},{8,0},{9,1},... | collective-permute-start | bytes 2506760 | tf_op jit(solution)/shard_map/ppermute | solution.py:58
  31.2 6.2 %collective-permute-start.7 = (bf16[544,768]{1,0:T(8,128)(2,1)S(1)}, bf16[544,768]{1,0:T(8,128)(2,1)S(1)}, u32[]{:S(2)}, u32[]{:S(2)}) collective-permute-start(bf16[544,768]{1,0:T(8,128)(2,1)S(1)} %collective-permute-done.1.refs_1_.refs_2_.refs_6_), channel_id=1, source_target_pairs={{0,8},{1,9},{2,10},{3,11},{4,12},{5,13},{6,14},{7,15},{8,0},{9,1},... | collective-permute-start | bytes 2506760 | tf_op jit(solution)/shard_map/ppermute | solution.py:58
  31.7 14.2 %collective-permute-start.5 = (bf16[544,768]{1,0:T(8,128)(2,1)S(1)}, bf16[544,768]{1,0:T(8,128)(2,1)S(1)}, u32[]{:S(2)}, u32[]{:S(2)}) collective-permute-start(bf16[544,768]{1,0:T(8,128)(2,1)S(1)} %collective-permute-done.refs_0_.refs_1_.refs_5_), channel_id=1, source_target_pairs={{0,16},{1,17},{2,18},{3,19},{4,20},{5,21},{6,22},{7,23},{8,56},{9,... | collective-permute-start | bytes 2506760 | tf_op jit(solution)/shard_map/ppermute | solution.py:58
  33.8 12.0 %collective-permute-start.9 = (bf16[256,384]{1,0:T(8,128)(2,1)S(1)}, bf16[256,384]{1,0:T(8,128)(2,1)S(1)}, u32[]{:S(2)}, u32[]{:S(2)}) collective-permute-start(bf16[256,384]{1,0:T(8,128)(2,1)S(1)} %get-tuple-element.78), channel_id=1, source_target_pairs={{0,1},{1,2},{2,3},{3,0},{4,5},{5,6},{6,7},{7,4},{8,11},{9,8},{10,9... | collective-permute-start | bytes 589832 | tf_op jit(solution)/shard_map/ppermute | solution.py:58
  34.6 11.3 %collective-permute-start.10 = (bf16[256,384]{1,0:T(8,128)(2,1)S(1)}, bf16[256,384]{1,0:T(8,128)(2,1)S(1)}, u32[]{:S(2)}, u32[]{:S(2)}) collective-permute-start(bf16[256,384]{1,0:T(8,128)(2,1)S(1)} %get-tuple-element.79), channel_id=1, source_target_pairs={{0,3},{1,0},{2,1},{3,2},{4,7},{5,4},{6,5},{7,6},{8,9},{9,10},{10,1... | collective-permute-start | bytes 589832 | tf_op jit(solution)/shard_map/ppermute | solution.py:58
  35.4 10.5 %collective-permute-start.11 = (bf16[256,384]{1,0:T(8,128)(2,1)S(1)}, bf16[256,384]{1,0:T(8,128)(2,1)S(1)}, u32[]{:S(2)}, u32[]{:S(2)}) collective-permute-start(bf16[256,384]{1,0:T(8,128)(2,1)S(1)} %get-tuple-element.80), channel_id=1, source_target_pairs={{0,2},{1,3},{2,0},{3,1},{4,6},{5,7},{6,4},{7,5},{8,10},{9,11},{10,... | collective-permute-start | bytes 589832 | tf_op jit(solution)/shard_map/ppermute | solution.py:58
  45.9 2.4 %collective-permute-start.12 = (bf16[544,768]{1,0:T(8,128)(2,1)S(1)}, bf16[544,768]{1,0:T(8,128)(2,1)S(1)}, u32[]{:S(2)}, u32[]{:S(2)}) collective-permute-start(bf16[544,768]{1,0:T(8,128)(2,1)S(1)} %collective-permute-done.5.refs_0_.refs_3_.refs_7_), channel_id=1, source_target_pairs={{0,8},{1,9},{2,10},{3,11},{4,12},{5,13},{6,14},{7,15},{8,0},{9,1},... | collective-permute-start | bytes 2506760 | tf_op jit(solution)/shard_map/ppermute | solution.py:58
  46.0 6.1 %collective-permute-start.13 = (bf16[128,768]{1,0:T(8,128)(2,1)S(1)}, bf16[128,768]{1,0:T(8,128)(2,1)S(1)}, u32[]{:S(2)}, u32[]{:S(2)}) collective-permute-start(bf16[128,768]{1,0:T(8,128)(2,1)S(1)} %prompt.1), channel_id=1, source_target_pairs={{0,64},{1,65},{2,66},{3,67},{4,68},{5,69},{6,70},{7,71},{8,72},{9,... | collective-permute-start | bytes 589832 | tf_op jit(solution)/shard_map/ppermute | solution.py:58
  48.3 3.7 %copy-start.1 = (bf16[384,3072]{1,0:T(8,128)(2,1)S(1)}, bf16[384,3072]{1,0:T(8,128)(2,1)}, u32[]{:S(2)}) copy-start(bf16[384,3072]{1,0:T(8,128)(2,1)} %w.1) | copy-start | bytes 7077892
  51.3 6.4 %copy-start.6 = (s32[4]{0:T(128)S(1)}, s32[4]{0:T(128)}, u32[]{:S(2)}) copy-start(s32[4]{0:T(128)} %start_ref.1) | copy-start | bytes 52
  51.3 6.4 %copy-start.7 = (s32[4]{0:T(128)S(1)}, s32[4]{0:T(128)}, u32[]{:S(2)}) copy-start(s32[4]{0:T(128)} %length_ref.1) | copy-start | bytes 52
  52.9 7.6 %collective-permute-start.14 = (bf16[384,1536]{1,0:T(8,128)(2,1)S(1)}, bf16[384,1536]{1,0:T(8,128)(2,1)S(1)}, u32[]{:S(2)}, u32[]{:S(2)}) collective-permute-start(bf16[384,1536]{1,0:T(8,128)(2,1)S(1)} %get-tuple-element.90), channel_id=1, source_target_pairs={{0,8},{1,9},{2,10},{3,11},{4,12},{5,13},{6,14},{7,15},{8,0},{9,1},... | collective-permute-start | bytes 3538952 | tf_op jit(solution)/shard_map/ppermute | solution.py:58
  54.5 3.2 %collective-permute-start.16 = (bf16[128,768]{1,0:T(8,128)(2,1)S(1)}, bf16[128,768]{1,0:T(8,128)(2,1)S(1)}, u32[]{:S(2)}, u32[]{:S(2)}) collective-permute-start(bf16[128,768]{1,0:T(8,128)(2,1)S(1)} %collective-permute-done.13.refs_12_), channel_id=1, source_target_pairs={{0,8},{1,9},{2,10},{3,11},{4,12},{5,13},{6,14},{7,15},{8,0},{9,1},... | collective-permute-start | bytes 589832 | tf_op jit(solution)/shard_map/ppermute | solution.py:58
  55.3 13.2 %collective-permute-start.15 = (bf16[512,512]{1,0:T(8,128)(2,1)S(1)}, bf16[512,512]{1,0:T(8,128)(2,1)S(1)}, u32[]{:S(2)}, u32[]{:S(2)}) collective-permute-start(bf16[512,512]{1,0:T(8,128)(2,1)S(1)} %far_other.1), channel_id=1, source_target_pairs={{0,64},{1,65},{2,66},{3,67},{4,68},{5,69},{6,70},{7,71},{8,72},{9,... | collective-permute-start | bytes 1572872 | tf_op jit(solution)/shard_map/ppermute | solution.py:58
  56.6 23.7 %collective-permute-start.24 = (bf16[384,1536]{1,0:T(8,128)(2,1)S(1)}, bf16[384,1536]{1,0:T(8,128)(2,1)S(1)}, u32[]{:S(2)}, u32[]{:S(2)}) collective-permute-start(bf16[384,1536]{1,0:T(8,128)(2,1)S(1)} %get-tuple-element.112.refs_9_), channel_id=1, source_target_pairs={{0,1},{1,2},{2,3},{3,0},{4,5},{5,6},{6,7},{7,4},{8,11},{9,8},{10,9... | collective-permute-start | bytes 3538952 | tf_op jit(solution)/shard_map/ppermute | solution.py:58
  69.6 5.4 %collective-permute-start.17 = (bf16[128,384]{1,0:T(8,128)(2,1)S(1)}, bf16[128,384]{1,0:T(8,128)(2,1)S(1)}, u32[]{:S(2)}, u32[]{:S(2)}) collective-permute-start(bf16[128,384]{1,0:T(8,128)(2,1)S(1)} %get-tuple-element.108), channel_id=1, source_target_pairs={{0,1},{1,2},{2,3},{3,0},{4,5},{5,6},{6,7},{7,4},{8,11},{9,8},{10,9... | collective-permute-start | bytes 294920 | tf_op jit(solution)/shard_map/ppermute | solution.py:58
  70.8 7.5 %collective-permute-start.18 = (bf16[128,384]{1,0:T(8,128)(2,1)S(1)}, bf16[128,384]{1,0:T(8,128)(2,1)S(1)}, u32[]{:S(2)}, u32[]{:S(2)}) collective-permute-start(bf16[128,384]{1,0:T(8,128)(2,1)S(1)} %get-tuple-element.109), channel_id=1, source_target_pairs={{0,3},{1,0},{2,1},{3,2},{4,7},{5,4},{6,5},{7,6},{8,9},{9,10},{10,1... | collective-permute-start | bytes 294920 | tf_op jit(solution)/shard_map/ppermute | solution.py:58
  71.1 7.1 %collective-permute-start.19 = (bf16[128,384]{1,0:T(8,128)(2,1)S(1)}, bf16[128,384]{1,0:T(8,128)(2,1)S(1)}, u32[]{:S(2)}, u32[]{:S(2)}) collective-permute-start(bf16[128,384]{1,0:T(8,128)(2,1)S(1)} %get-tuple-element.110), channel_id=1, source_target_pairs={{0,2},{1,3},{2,0},{3,1},{4,6},{5,7},{6,4},{7,5},{8,10},{9,11},{10,... | collective-permute-start | bytes 294920 | tf_op jit(solution)/shard_map/ppermute | solution.py:58
  73.0 7.3 %collective-permute-start.20 = (bf16[128,384]{1,0:T(8,128)(2,1)S(1)}, bf16[128,384]{1,0:T(8,128)(2,1)S(1)}, u32[]{:S(2)}, u32[]{:S(2)}) collective-permute-start(bf16[128,384]{1,0:T(8,128)(2,1)S(1)} %get-tuple-element.107.refs_0_), channel_id=1, source_target_pairs={{0,8},{1,9},{2,10},{3,11},{4,12},{5,13},{6,14},{7,15},{8,0},{9,1},... | collective-permute-start | bytes 294920 | tf_op jit(solution)/shard_map/ppermute | solution.py:58
  75.0 5.3 %collective-permute-start.21 = (bf16[128,384]{1,0:T(8,128)(2,1)S(1)}, bf16[128,384]{1,0:T(8,128)(2,1)S(1)}, u32[]{:S(2)}, u32[]{:S(2)}) collective-permute-start(bf16[128,384]{1,0:T(8,128)(2,1)S(1)} %collective-permute-done.17.refs_1_), channel_id=1, source_target_pairs={{0,8},{1,9},{2,10},{3,11},{4,12},{5,13},{6,14},{7,15},{8,0},{9,1},... | collective-permute-start | bytes 294920 | tf_op jit(solution)/shard_map/ppermute | solution.py:58
  78.3 2.1 %collective-permute-start.22 = (bf16[128,384]{1,0:T(8,128)(2,1)S(1)}, bf16[128,384]{1,0:T(8,128)(2,1)S(1)}, u32[]{:S(2)}, u32[]{:S(2)}) collective-permute-start(bf16[128,384]{1,0:T(8,128)(2,1)S(1)} %collective-permute-done.18.refs_2_), channel_id=1, source_target_pairs={{0,8},{1,9},{2,10},{3,11},{4,12},{5,13},{6,14},{7,15},{8,0},{9,1},... | collective-permute-start | bytes 294920 | tf_op jit(solution)/shard_map/ppermute | solution.py:58
  78.3 3.0 %collective-permute-start.23 = (bf16[128,384]{1,0:T(8,128)(2,1)S(1)}, bf16[128,384]{1,0:T(8,128)(2,1)S(1)}, u32[]{:S(2)}, u32[]{:S(2)}) collective-permute-start(bf16[128,384]{1,0:T(8,128)(2,1)S(1)} %collective-permute-done.19.refs_3_), channel_id=1, source_target_pairs={{0,8},{1,9},{2,10},{3,11},{4,12},{5,13},{6,14},{7,15},{8,0},{9,1},... | collective-permute-start | bytes 294920 | tf_op jit(solution)/shard_map/ppermute | solution.py:58
  83.0 7.7 %collective-permute-start.25 = (bf16[64,1536]{1,0:T(8,128)(2,1)S(1)}, bf16[64,1536]{1,0:T(8,128)(2,1)S(1)}, u32[]{:S(2)}, u32[]{:S(2)}) collective-permute-start(bf16[64,1536]{1,0:T(8,128)(2,1)S(1)} %get-tuple-element.114), channel_id=1, source_target_pairs={{0,4},{1,5},{2,6},{3,7},{4,0},{5,1},{6,2},{7,3},{8,12},{9,13},{10,... | collective-permute-start | bytes 589832 | tf_op jit(solution)/shard_map/ppermute | solution.py:58
  86.0 4.7 %collective-permute-start.26 = (bf16[64,1536]{1,0:T(8,128)(2,1)S(1)}, bf16[64,1536]{1,0:T(8,128)(2,1)S(1)}, u32[]{:S(2)}, u32[]{:S(2)}) collective-permute-start(bf16[64,1536]{1,0:T(8,128)(2,1)S(1)} %get-tuple-element.115), channel_id=1, source_target_pairs={{0,8},{1,9},{2,10},{3,11},{4,12},{5,13},{6,14},{7,15},{8,0},{9,1},... | collective-permute-start | bytes 589832 | tf_op jit(solution)/shard_map/ppermute | solution.py:58
  86.7 8.8 %collective-permute-start.27 = (bf16[64,1536]{1,0:T(8,128)(2,1)S(1)}, bf16[64,1536]{1,0:T(8,128)(2,1)S(1)}, u32[]{:S(2)}, u32[]{:S(2)}) collective-permute-start(bf16[64,1536]{1,0:T(8,128)(2,1)S(1)} %get-tuple-element.116), channel_id=1, source_target_pairs={{0,12},{1,13},{2,14},{3,15},{4,8},{5,9},{6,10},{7,11},{8,4},{9,5},... | collective-permute-start | bytes 589832 | tf_op jit(solution)/shard_map/ppermute | solution.py:58

commit v2 on v1

--- a/solution.py
+++ b/solution.py
@@ -12,6 +12,7 @@
 HEADS = 3
 GROUP = HEADS * HD
 SUB = 256
+DIGITS = 16
 ROWS = 512
 TEXT = 32
 SCALE = HD ** (-0.5) * 1.4426950408889634
@@ -19,6 +20,7 @@
 AXES = ("seq", "aud")
 NT = (((1,), (1,)), ((), ()))
 NN = (((1,), (0,)), ((), ()))
+TN = (((0,), (0,)), ((), ()))
 F32 = jnp.float32
 BF16 = jnp.bfloat16
 PARAMS = pltpu.CompilerParams(vmem_limit_bytes=20 * 2**20)
@@ -30,7 +32,7 @@
     return pl.CostEstimate(flops=int(us * 1.15e9), bytes_accessed=1024, transcendentals=0)
 
 
-TIMES = dict(near_mine=2.4, near_other=2.4, mid=8.0, far_other=2.8, far_mine=26.0, side=2.7)
+TIMES = dict(near_mine=2.4, near_other=2.4, mid=8.0, far_other=2.8, far_mine=26.0, side=20.0, join=20.0)
 SMEM = pl.BlockSpec(memory_space=pltpu.SMEM)
 VMEM = pl.BlockSpec(memory_space=pltpu.VMEM)
 HBM = pl.BlockSpec(memory_space=pltpu.HBM)
@@ -196,9 +198,10 @@
 
 
 def undigit(table, head, first, count):
-    row = lax.broadcasted_iota(jnp.int32, (HD, HD), 0)
+    row = lax.broadcasted_iota(jnp.int32, (DIGITS, HD), 0)
     picked = (row % HEADS == head) & (row >= first * HEADS) & (row < (first + count) * HEADS)
-    return lax.dot_general(table, picked.astype(F32).astype(BF16), NN, preferred_element_type=F32)
+    picked = picked.astype(F32).astype(BF16)
+    return lax.dot_general(table, picked, TN, preferred_element_type=F32)
 
 
 def blend(parts):
@@ -252,7 +255,9 @@
                     for j in range(3):
                         outs[3 * number + j][rows, cols] = result[j]
             if packed:
-                outs[number][rows, GROUP:] = table.astype(BF16)
+                below = pl.ds(ROWS + start // SUB * DIGITS, DIGITS)
+                outs[number][below, :SUB] = jnp.transpose(table)[:DIGITS].astype(BF16)
+                outs[number][below, SUB:] = jnp.zeros((DIGITS, GROUP - SUB), BF16)
 
 
 def flash(name, arrays, queries, priors=None, packed=False):
@@ -261,7 +266,7 @@
     n_priors = len(priors[0])
     flat = [ref for parts in priors for part in parts for ref in part]
     if packed:
-        shapes = [jax.ShapeDtypeStruct((ROWS, GROUP + HD), BF16)] * n_sets
+        shapes = [jax.ShapeDtypeStruct((ROWS + ROWS // SUB * DIGITS, GROUP), BF16)] * n_sets
     else:
         shapes = [jax.ShapeDtypeStruct((ROWS, GROUP), F32)] * (3 * n_sets)
     outs = pl.pallas_call(
@@ -336,16 +341,18 @@
 
 def join_body(here, *refs):
     mine, packed_ref, side_ref, outs, joined = refs[:3], refs[3], refs[4], refs[5:9], refs[9]
-    for head in range(HEADS):
-        cols = pl.ds(head * HD, HD)
-        table = packed_ref[:, GROUP:]
-        other = (
-            packed_ref[:, cols].astype(F32),
-            undigit(table, head, 0, 3),
-            undigit(table, head, 3, 2),
-        )
-        mixed, _, weight = blend([tuple(ref[:, cols] for ref in mine), other])
-        joined[:, cols] = (mixed / weight + side_ref[:, cols]).astype(BF16)
+    for start in range(0, ROWS, SUB):
+        rows = pl.ds(start, SUB)
+        table = packed_ref[pl.ds(ROWS + start // SUB * DIGITS, DIGITS), :SUB]
+        for head in range(HEADS):
+            cols = pl.ds(head * HD, HD)
+            other = (
+                packed_ref[rows, cols].astype(F32),
+                undigit(table, head, 0, 3),
+                undigit(table, head, 3, 2),
+            )
+            mixed, _, weight = blend([tuple(ref[rows, cols] for ref in mine), other])
+            joined[rows, cols] = (mixed / weight + side_ref[rows, cols]).astype(BF16)
     core, y_hi, z = here[0], here[3], here[4]
     step = 1 - 2 * core
     for out, shift in zip(outs, (0, step, -step, 2)):
@@ -364,7 +371,7 @@
         out_specs=[VMEM] * 4,
         scratch_shapes=[pltpu.VMEM((ROWS, GROUP), BF16)],
         compiler_params=PARAMS,
-        cost_estimate=COST,
+        cost_estimate=lasting(TIMES["join"]),
         name="join",
     )(here, *mine, packed, side_part)
 
@@ -466,18 +473,18 @@
         (kv3, mid_mine, mid_other, *audios)
     )
     kv3_c = send(kv3, CORE)
+    w0, w1, w2 = split(here, w_out, after(came, *mid_mine))
+    w3 = send(w1, Z_A)
+    w2 = send(w2, CORE)
     text = prompt(own, kv1, kv2, kv3)
     text_y = send(text, Y_LO)
     (packed,) = flash(
-        "far_other", [kv3, kv3_c], [asked], [[near_other, mid_other]], packed=True
-    )
-    packed, text_y = lax.optimization_barrier((packed, text_y))
+        "far_other", [kv3, kv3_c], [after(asked, w0)], [[near_other, mid_other]], packed=True
+    )
     got = send(packed, Y_LO)
-    w0, w1, w2 = split(here, w_out, after(came, packed))
-    w3 = send(w1, Z_A)
-    w2 = send(w2, CORE)
+    text_y = after(text_y, packed)
     text_yc = send(text_y, CORE)
-    (far_mine,) = flash("far_mine", [kv3, kv3_c], [after(video_q, packed, w2)], [[near_mine, mid_mine]])
+    (far_mine,) = flash("far_mine", [kv3, kv3_c], [after(video_q, packed)], [[near_mine, mid_mine]])
     side_part = side(
         here,
         block_start,

time: 97 us -> 92.6 us (0.955)
  waiting for transfers between devices: 28.1 us -> 25.9 us
  starting transfers between devices: 36.1 us -> 34.3 us
    ppermute x28, waiting for transfers between devices: 28.1 us -> 25.9 us  [send(): return lax.ppermute(array, AXES, route)]
    ppermute x28, starting transfers between devices: 36.1 us -> 34.3 us  [send(): return lax.ppermute(array, AXES, route)]
  transfers between devices with their start and end apart: 28 -> 28, of which waited for: 10 -> 9; matrix products, arithmetic and copies ran while one was open for 1% -> 1% of each run, Pallas kernels for 28% -> 30%
where the time goes in v2:
time: 92.6 us; the launch traced here: 92.4 us
  starting transfers between devices  34.3 us (37%)
  Pallas kernels  30.5 us (33%)
  waiting for transfers between devices  25.9 us (28%)
    ppermute x28, starting transfers between devices, send(): return lax.ppermute(array, AXES, route)  34.3 us
    ppermute x28, waiting for transfers between devices, send(): return lax.ppermute(array, AXES, route)  25.9 us
    pallas_call x5, Pallas kernels, flash(): pl.pallas_call(functools.partial(flash_body, n_arrays, n_sets, n_priors,...  18.4 us
    pallas_call x1, Pallas kernels, stage(): pl.pallas_call(stage_body, out_shape=jax.ShapeDtypeStruct((ROWS + TEXT, 2...  2.85 us
    pallas_call x1, Pallas kernels, side(): pl.pallas_call(side_body, out_shape=jax.ShapeDtypeStruct(q.shape, F32), g...  2.73 us
  transfers between devices with their start and end apart: 28, of which 9 were waited for; matrix products, arithmetic and copies ran while one was open for 1% of the time, Pallas kernels for 30%

profile of v2, /device:TPU:1, one launch (start us, length us, event | category | flops | bytes accessed | tf_op | source)
XLA Modules:
  0.0 92.4 jit_solution(1223083264986635796)
XLA Ops:
  0.0 4.7 %collective-permute-start.8 = (bf16[384,3072]{1,0:T(8,128)(2,1)}, bf16[384,3072]{1,0:T(8,128)(2,1)S(1)}, u32[]{:S(2)}, u32[]{:S(2)}) collective-permute-start(bf16[384,3072]{1,0:T(8,128)(2,1)} %w.1), channel_id=1, source_target_pairs={{0,1},{1,2},{2,3},{3,0},{4,5},{5,6},{6,7},{7,4},{8,11},{9,8},{10,9... | collective-permute-start | bytes 7077896 | tf_op jit(solution)/shard_map/ppermute | solution.py:60
  4.7 0.6 stack.23._.here
  5.3 2.9 %stage.1.refs_0_.refs_4_ = bf16[544,768]{1,0:T(8,128)(2,1)} custom-call(s32[5]{0:T(128)} %stack.23._.here, bf16[512,384]{1,0:T(8,128)(2,1)} %k.1, bf16[512,384]{1,0:T(8,128)(2,1)} %v.1, bf16[32,384]{1,0:T(8,128)(2,1)} %tk.1, bf16[32,384]{1,0:T(8,128)(2,1)} %tv.1), custom_call_target="tpu_custom_call" | custom-call | flops 1024 | bytes 1024 | tf_op jit(solution)/shard_map/stage/pallas_call | solution.py:92
  8.1 0.1 collective-permute-start.2
  8.2 2.5 %collective-permute-start = (bf16[544,768]{1,0:T(8,128)(2,1)}, bf16[544,768]{1,0:T(8,128)(2,1)S(1)}, u32[]{:S(2)}, u32[]{:S(2)}) collective-permute-start(bf16[544,768]{1,0:T(8,128)(2,1)} %stage.1.refs_0_.refs_4_), channel_id=1, source_target_pairs={{0,16},{1,17},{2,18},{3,19},{4,20},{5,21},{6,22},{7,23},{8,56},{9,... | collective-permute-start | bytes 2506760 | tf_op jit(solution)/shard_map/ppermute | solution.py:60
  10.8 1.3 %collective-permute-start.3 = (bf16[512,384]{1,0:T(8,128)(2,1)S(1)}, bf16[512,384]{1,0:T(8,128)(2,1)S(1)}, u32[]{:S(2)}, u32[]{:S(2)}) collective-permute-start(bf16[512,384]{1,0:T(8,128)(2,1)S(1)} %copy-done.5), channel_id=1, source_target_pairs={{0,64},{1,65},{2,66},{3,67},{4,68},{5,69},{6,70},{7,71},{8,72},{9,... | collective-permute-start | bytes 1179656 | tf_op jit(solution)/shard_map/ppermute | solution.py:60
  12.1 0.6 lend.1
  12.7 2.0 %collective-permute-start.4 = (bf16[128,1536]{1,0:T(8,128)(2,1)S(1)}, bf16[128,1536]{1,0:T(8,128)(2,1)S(1)}, u32[]{:S(2)}, u32[]{:S(2)}) collective-permute-start(bf16[128,1536]{1,0:T(8,128)(2,1)S(1)} %lend.1), channel_id=1, source_target_pairs={{0,68},{1,69},{2,70},{3,71},{4,64},{5,65},{6,66},{7,67},{8,76},{9,... | collective-permute-start | bytes 1179656 | tf_op jit(solution)/shard_map/ppermute | solution.py:60
  14.7 2.4 %near_mine.1 = (f32[512,384]{1,0:T(8,128)S(1)}, f32[512,384]{1,0:T(8,128)S(1)}, f32[512,384]{1,0:T(8,128)S(1)}) custom-call(bf16[544,768]{1,0:T(8,128)(2,1)S(1)} %copy-done, bf16[544,768]{1,0:T(8,128)(2,1)S(1)} %collective-permute-done.2.refs_1_.refs_8_, bf16[512,384]{1,0:T(8,128)(2,1)S(1)} %copy-done.5), custom_call_target="tpu_custom_call" | custom-call | flops 2760000000 | bytes 1024 | tf_op jit(solution)/shard_map/near_mine/pallas_call | solution.py:272
  17.1 3.1 %collective-permute-done.3.refs_2_.refs_5_ = bf16[512,384]{1,0:T(8,128)(2,1)S(1)} collective-permute-done((bf16[512,384]{1,0:T(8,128)(2,1)S(1)}, bf16[512,384]{1,0:T(8,128)(2,1)S(1)}, u32[]{:S(2)}, u32[]{:S(2)}) %collective-permute-start.3) | collective-permute-done | bytes 393248 | tf_op jit(solution)/shard_map/ppermute | solution.py:60
  20.2 2.3 %near_other.1 = (f32[512,384]{1,0:T(8,128)S(1)}, f32[512,384]{1,0:T(8,128)S(1)}, f32[512,384]{1,0:T(8,128)S(1)}) custom-call(bf16[544,768]{1,0:T(8,128)(2,1)S(1)} %copy-done, bf16[544,768]{1,0:T(8,128)(2,1)S(1)} %collective-permute-done.2.refs_1_.refs_8_, bf16[512,384]{1,0:T(8,128)(2,1)S(1)} %collective-permute-done.3.refs_2_.refs_5_), custom_call_target="tpu_custom_call" | custom-call | flops 2760000000 | bytes 1024 | tf_op jit(solution)/shard_map/near_other/pallas_call | solution.py:272
  22.5 0.6 collective-permute-done.4.lent
  23.2 4.9 %collective-permute-done.refs_0_.refs_1_.refs_5_ = bf16[544,768]{1,0:T(8,128)(2,1)S(1)} collective-permute-done((bf16[544,768]{1,0:T(8,128)(2,1)}, bf16[544,768]{1,0:T(8,128)(2,1)S(1)}, u32[]{:S(2)}, u32[]{:S(2)}) %collective-permute-start) | collective-permute-done | bytes 835616 | tf_op jit(solution)/shard_map/ppermute | solution.py:60
  28.1 3.1 %collective-permute-done.1.refs_1_.refs_2_.refs_6_ = bf16[544,768]{1,0:T(8,128)(2,1)S(1)} collective-permute-done((bf16[544,768]{1,0:T(8,128)(2,1)}, bf16[544,768]{1,0:T(8,128)(2,1)S(1)}, u32[]{:S(2)}, u32[]{:S(2)}) %collective-permute-start.1) | collective-permute-done | bytes 835616 | tf_op jit(solution)/shard_map/ppermute | solution.py:60
  31.2 0.5 collective-permute-start.7
  31.7 1.5 %collective-permute-start.5 = (bf16[544,768]{1,0:T(8,128)(2,1)S(1)}, bf16[544,768]{1,0:T(8,128)(2,1)S(1)}, u32[]{:S(2)}, u32[]{:S(2)}) collective-permute-start(bf16[544,768]{1,0:T(8,128)(2,1)S(1)} %collective-permute-done.refs_0_.refs_1_.refs_5_), channel_id=1, source_target_pairs={{0,16},{1,17},{2,18},{3,19},{4,20},{5,21},{6,22},{7,23},{8,56},{9,... | collective-permute-start | bytes 2506760 | tf_op jit(solution)/shard_map/ppermute | solution.py:60
  33.2 0.6 deal.1
  33.8 0.5 collective-permute-start.10
  34.3 1.8 %collective-permute-start.11 = (bf16[256,384]{1,0:T(8,128)(2,1)S(1)}, bf16[256,384]{1,0:T(8,128)(2,1)S(1)}, u32[]{:S(2)}, u32[]{:S(2)}) collective-permute-start(bf16[256,384]{1,0:T(8,128)(2,1)S(1)} %get-tuple-element.79), channel_id=1, source_target_pairs={{0,2},{1,3},{2,0},{3,1},{4,6},{5,7},{6,4},{7,5},{8,10},{9,11},{10,... | collective-permute-start | bytes 589832 | tf_op jit(solution)/shard_map/ppermute | solution.py:60
  36.1 2.0 %collective-permute-start.9 = (bf16[256,384]{1,0:T(8,128)(2,1)S(1)}, bf16[256,384]{1,0:T(8,128)(2,1)S(1)}, u32[]{:S(2)}, u32[]{:S(2)}) collective-permute-start(bf16[256,384]{1,0:T(8,128)(2,1)S(1)} %get-tuple-element.77), channel_id=1, source_target_pairs={{0,1},{1,2},{2,3},{3,0},{4,5},{5,6},{6,7},{7,4},{8,11},{9,8},{10,9... | collective-permute-start | bytes 589832 | tf_op jit(solution)/shard_map/ppermute | solution.py:60
  38.0 8.1 %mid.1 = (f32[512,384]{1,0:T(8,128)S(1)}, f32[512,384]{1,0:T(8,128)S(1)}, f32[512,384]{1,0:T(8,128)S(1)}, f32[512,384]{1,0:T(8,128)S(1)}, f32[512,384]{1,0:T(8,128)S(1)}, /*index=5*/f32[512,384]{1,0:T(8,128)S(1)}) custom-call(bf16[544,768]{1,0:T(8,128)(2,1)S(1)} %collective-permute-done.refs_0_.refs_1_.refs_5_, ...), custom_call_target="tpu_custom_call" | custom-call | flops 9200000000 | bytes 1024 | tf_op jit(solution)/shard_map/mid/pallas_call | solution.py:272
  46.2 0.5 collective-permute-start.12
  47.3 1.4 %collective-permute-start.14 = (bf16[128,768]{1,0:T(8,128)(2,1)S(1)}, bf16[128,768]{1,0:T(8,128)(2,1)S(1)}, u32[]{:S(2)}, u32[]{:S(2)}) collective-permute-start(bf16[128,768]{1,0:T(8,128)(2,1)S(1)} %prompt.1), channel_id=1, source_target_pairs={{0,64},{1,65},{2,66},{3,67},{4,68},{5,69},{6,70},{7,71},{8,72},{9,... | collective-permute-start | bytes 589832 | tf_op jit(solution)/shard_map/ppermute | solution.py:60
  48.7 0.3 copy-done.1
  49.0 0.8 split.1
  49.8 0.3 collective-permute-start.23
  50.0 0.2 collective-permute-start.24
  50.2 2.8 %far_other.1 = bf16[544,384]{1,0:T(8,128)(2,1)S(1)} custom-call(bf16[544,768]{1,0:T(8,128)(2,1)S(1)} %collective-permute-done.5.refs_0_.refs_3_.refs_7_, bf16[544,768]{1,0:T(8,128)(2,1)S(1)} %collective-permute-done.12.refs_1_.refs_11_, bf16[512,384]{1,0:T(8,128)(2,1)S(1)} %collective-permute-done.3.refs_2_.refs_5_, ...), custom_call_target="tpu_custom_call" | custom-call | flops 3220000000 | bytes 1024 | tf_op jit(solution)/shard_map/far_other/pallas_call | solution.py:272
  53.0 1.3 %collective-permute-start.13 = (bf16[544,384]{1,0:T(8,128)(2,1)S(1)}, bf16[544,384]{1,0:T(8,128)(2,1)S(1)}, u32[]{:S(2)}, u32[]{:S(2)}) collective-permute-start(bf16[544,384]{1,0:T(8,128)(2,1)S(1)} %far_other.1), channel_id=1, source_target_pairs={{0,64},{1,65},{2,66},{3,67},{4,68},{5,69},{6,70},{7,71},{8,72},{9,... | collective-permute-start | bytes 1253384 | tf_op jit(solution)/shard_map/ppermute | solution.py:60
  54.4 0.5 collective-permute-start.15
  54.9 2.7 %far_mine.1 = (f32[512,384]{1,0:T(8,128)S(1)}, f32[512,384]{1,0:T(8,128)S(1)}, f32[512,384]{1,0:T(8,128)S(1)}) custom-call(bf16[544,768]{1,0:T(8,128)(2,1)S(1)} %collective-permute-done.5.refs_0_.refs_3_.refs_7_, bf16[544,768]{1,0:T(8,128)(2,1)S(1)} %collective-permute-done.12.refs_1_.refs_11_, bf16[512,384]{1,0:T(8,128)(2,1)S(1)} %copy-done.5, ...), custom_call_target="tpu_custom_call" | custom-call | flops 29899999232 | bytes 1024 | tf_op jit(solution)/shard_map/far_mine/pallas_call | solution.py:272
  57.6 2.7 %side.1.refs_4_ = f32[512,384]{1,0:T(8,128)S(1)} custom-call(s32[5]{0:T(128)S(1)} %copy-done.4, s32[4]{0:T(128)S(1)} %copy-done.6, s32[4]{0:T(128)S(1)} %copy-done.7, s32[1]{0:T(128)S(6)} %copy.12.prompt_ref, bf16[512,384]{1,0:T(8,128)(2,1)S(1)} %copy-done.5, bf16[256,384]{1,0:T(8,128)(2,1)S(1)} %get-tuple-element.100.refs_0_, ...), custom_call_target="tpu_custom_call" | custom-call | flops 23000000512 | bytes 1024 | tf_op jit(solution)/shard_map/side/pallas_call | solution.py:330
  60.4 3.8 %collective-permute-done.13.refs_3_ = bf16[544,384]{1,0:T(8,128)(2,1)S(1)} collective-permute-done((bf16[544,384]{1,0:T(8,128)(2,1)S(1)}, bf16[544,384]{1,0:T(8,128)(2,1)S(1)}, u32[]{:S(2)}, u32[]{:S(2)}) %collective-permute-start.13) | collective-permute-done | bytes 417824 | tf_op jit(solution)/shard_map/ppermute | solution.py:60
  64.2 1.2 %join.1 = (bf16[128,384]{1,0:T(8,128)(2,1)S(1)}, bf16[128,384]{1,0:T(8,128)(2,1)S(1)}, bf16[128,384]{1,0:T(8,128)(2,1)S(1)}, bf16[128,384]{1,0:T(8,128)(2,1)S(1)}) custom-call(s32[5]{0:T(128)S(1)} %copy-done.4, f32[512,384]{1,0:T(8,128)S(1)} %get-tuple-element.97.refs_0_, f32[512,384]{1,0:T(8,128)S(1)} %get-tuple-element.98.refs_1_, ...), custom_call_target="tpu_custom_call" | custom-call | flops 23000000512 | bytes 1024 | tf_op jit(solution)/shard_map/join/pallas_call | solution.py:367
  65.5 2.0 %collective-permute-start.17 = (bf16[128,384]{1,0:T(8,128)(2,1)S(1)}, bf16[128,384]{1,0:T(8,128)(2,1)S(1)}, u32[]{:S(2)}, u32[]{:S(2)}) collective-permute-start(bf16[128,384]{1,0:T(8,128)(2,1)S(1)} %get-tuple-element.107), channel_id=1, source_target_pairs={{0,3},{1,0},{2,1},{3,2},{4,7},{5,4},{6,5},{7,6},{8,9},{9,10},{10,1... | collective-permute-start | bytes 294920 | tf_op jit(solution)/shard_map/ppermute | solution.py:60
  67.6 1.7 %collective-permute-start.18 = (bf16[128,384]{1,0:T(8,128)(2,1)S(1)}, bf16[128,384]{1,0:T(8,128)(2,1)S(1)}, u32[]{:S(2)}, u32[]{:S(2)}) collective-permute-start(bf16[128,384]{1,0:T(8,128)(2,1)S(1)} %get-tuple-element.108), channel_id=1, source_target_pairs={{0,2},{1,3},{2,0},{3,1},{4,6},{5,7},{6,4},{7,5},{8,10},{9,11},{10,... | collective-permute-start | bytes 294920 | tf_op jit(solution)/shard_map/ppermute | solution.py:60
  69.3 1.1 %collective-permute-start.19 = (bf16[128,384]{1,0:T(8,128)(2,1)S(1)}, bf16[128,384]{1,0:T(8,128)(2,1)S(1)}, u32[]{:S(2)}, u32[]{:S(2)}) collective-permute-start(bf16[128,384]{1,0:T(8,128)(2,1)S(1)} %get-tuple-element.105.refs_0_), channel_id=1, source_target_pairs={{0,8},{1,9},{2,10},{3,11},{4,12},{5,13},{6,14},{7,15},{8,0},{9,1},... | collective-permute-start | bytes 294920 | tf_op jit(solution)/shard_map/ppermute | solution.py:60
  70.3 2.0 %collective-permute-start.20 = (bf16[128,384]{1,0:T(8,128)(2,1)S(1)}, bf16[128,384]{1,0:T(8,128)(2,1)S(1)}, u32[]{:S(2)}, u32[]{:S(2)}) collective-permute-start(bf16[128,384]{1,0:T(8,128)(2,1)S(1)} %collective-permute-done.16.refs_1_), channel_id=1, source_target_pairs={{0,8},{1,9},{2,10},{3,11},{4,12},{5,13},{6,14},{7,15},{8,0},{9,1},... | collective-permute-start | bytes 294920 | tf_op jit(solution)/shard_map/ppermute | solution.py:60
  72.3 0.5 collective-permute-start.21
  72.8 0.5 collective-permute-done.18.refs_3_
  73.3 2.5 %collective-permute-start.22 = (bf16[128,384]{1,0:T(8,128)(2,1)S(1)}, bf16[128,384]{1,0:T(8,128)(2,1)S(1)}, u32[]{:S(2)}, u32[]{:S(2)}) collective-permute-start(bf16[128,384]{1,0:T(8,128)(2,1)S(1)} %collective-permute-done.18.refs_3_), channel_id=1, source_target_pairs={{0,8},{1,9},{2,10},{3,11},{4,12},{5,13},{6,14},{7,15},{8,0},{9,1},... | collective-permute-start | bytes 294920 | tf_op jit(solution)/shard_map/ppermute | solution.py:60
  75.9 0.9 collective-permute-done.22.refs_7_
  76.8 1.8 %project.1 = (f32[64,1536]{1,0:T(8,128)S(1)}, bf16[64,1536]{1,0:T(8,128)(2,1)S(1)}, bf16[64,1536]{1,0:T(8,128)(2,1)S(1)}, bf16[64,1536]{1,0:T(8,128)(2,1)S(1)}) custom-call(bf16[128,384]{1,0:T(8,128)(2,1)S(1)} %get-tuple-element.105.refs_0_, bf16[128,384]{1,0:T(8,128)(2,1)S(1)} %collective-permute-done.16.refs_1_, ...), custom_call_target="tpu_custom_call" | custom-call | flops 1024 | bytes 1024 | tf_op jit(solution)/shard_map/project/pallas_call | solution.py:400
  78.6 3.0 %collective-permute-start.25 = (bf16[64,1536]{1,0:T(8,128)(2,1)S(1)}, bf16[64,1536]{1,0:T(8,128)(2,1)S(1)}, u32[]{:S(2)}, u32[]{:S(2)}) collective-permute-start(bf16[64,1536]{1,0:T(8,128)(2,1)S(1)} %get-tuple-element.112), channel_id=1, source_target_pairs={{0,4},{1,5},{2,6},{3,7},{4,0},{5,1},{6,2},{7,3},{8,12},{9,13},{10,... | collective-permute-start | bytes 589832 | tf_op jit(solution)/shard_map/ppermute | solution.py:60
  81.5 0.6 collective-permute-start.26
  82.2 4.1 %collective-permute-done.25.pair = bf16[64,1536]{1,0:T(8,128)(2,1)S(1)} collective-permute-done((bf16[64,1536]{1,0:T(8,128)(2,1)S(1)}, bf16[64,1536]{1,0:T(8,128)(2,1)S(1)}, u32[]{:S(2)}, u32[]{:S(2)}) %collective-permute-start.25) | collective-permute-done | bytes 196640 | tf_op jit(solution)/shard_map/ppermute | solution.py:60
  86.3 4.7 %collective-permute-done.27.both = bf16[64,1536]{1,0:T(8,128)(2,1)S(1)} collective-permute-done((bf16[64,1536]{1,0:T(8,128)(2,1)S(1)}, bf16[64,1536]{1,0:T(8,128)(2,1)S(1)}, u32[]{:S(2)}, u32[]{:S(2)}) %collective-permute-start.27) | collective-permute-done | bytes 196640 | tf_op jit(solution)/shard_map/ppermute | solution.py:60
  91.0 1.4 %total.1 = bf16[64,3072]{1,0:T(8,128)(2,1)} custom-call(s32[5]{0:T(128)S(1)} %copy-done.4, f32[64,1536]{1,0:T(8,128)S(1)} %get-tuple-element.111.keep, bf16[64,1536]{1,0:T(8,128)(2,1)S(1)} %collective-permute-done.25.pair, bf16[64,1536]{1,0:T(8,128)(2,1)S(1)} %collective-permute-done.26.core, bf16[64,1536]{1,0:T(8,128)(2,1)S(1)} %collective-permute-done.27.both), custom_call_target="tpu_custom_call" | custom-call | flops 1024 | bytes 1024 | tf_op jit(solution)/shard_map/total/pallas_call | solution.py:426
  (39 shorter events, 0.2 us)
Async XLA Ops:
  0.0 10.8 %copy-start.5 = (bf16[512,384]{1,0:T(8,128)(2,1)S(1)}, bf16[512,384]{1,0:T(8,128)(2,1)}, u32[]{:S(2)}) copy-start(bf16[512,384]{1,0:T(8,128)(2,1)} %q_ref) | copy-start | bytes 1179652
  0.0 12.1 %copy-start.2 = (bf16[64,3072]{1,0:T(8,128)(2,1)S(1)}, bf16[64,3072]{1,0:T(8,128)(2,1)}, u32[]{:S(2)}) copy-start(bf16[64,3072]{1,0:T(8,128)(2,1)} %ak.3) | copy-start | bytes 1179652
  0.0 12.1 %copy-start.3 = (bf16[64,3072]{1,0:T(8,128)(2,1)S(1)}, bf16[64,3072]{1,0:T(8,128)(2,1)}, u32[]{:S(2)}) copy-start(bf16[64,3072]{1,0:T(8,128)(2,1)} %av.3) | copy-start | bytes 1179652
  0.0 34.3 %collective-permute-start.8 = (bf16[384,3072]{1,0:T(8,128)(2,1)}, bf16[384,3072]{1,0:T(8,128)(2,1)S(1)}, u32[]{:S(2)}, u32[]{:S(2)}) collective-permute-start(bf16[384,3072]{1,0:T(8,128)(2,1)} %w.1), channel_id=1, source_target_pairs={{0,1},{1,2},{2,3},{3,0},{4,5},{5,6},{6,7},{7,4},{8,11},{9,8},{10,9... | collective-permute-start | bytes 7077896 | tf_op jit(solution)/shard_map/ppermute | solution.py:60
  5.3 6.8 %copy-start.4 = (s32[5]{0:T(128)S(1)}, s32[5]{0:T(128)}, u32[]{:S(2)}) copy-start(s32[5]{0:T(128)} %stack.23._.here) | copy-start | bytes 64
  8.1 6.6 %copy-start = (bf16[544,768]{1,0:T(8,128)(2,1)S(1)}, bf16[544,768]{1,0:T(8,128)(2,1)}, u32[]{:S(2)}) copy-start(bf16[544,768]{1,0:T(8,128)(2,1)} %stage.1.refs_0_.refs_4_) | copy-start | bytes 2506756
  8.1 4.6 %collective-permute-start.2 = (bf16[544,768]{1,0:T(8,128)(2,1)}, bf16[544,768]{1,0:T(8,128)(2,1)S(1)}, u32[]{:S(2)}, u32[]{:S(2)}) collective-permute-start(bf16[544,768]{1,0:T(8,128)(2,1)} %stage.1.refs_0_.refs_4_), channel_id=1, source_target_pairs={{0,8},{1,9},{2,10},{3,11},{4,12},{5,13},{6,14},{7,15},{8,0},{9,1},... | collective-permute-start | bytes 2506760 | tf_op jit(solution)/shard_map/ppermute | solution.py:60
  8.2 19.9 %collective-permute-start = (bf16[544,768]{1,0:T(8,128)(2,1)}, bf16[544,768]{1,0:T(8,128)(2,1)S(1)}, u32[]{:S(2)}, u32[]{:S(2)}) collective-permute-start(bf16[544,768]{1,0:T(8,128)(2,1)} %stage.1.refs_0_.refs_4_), channel_id=1, source_target_pairs={{0,16},{1,17},{2,18},{3,19},{4,20},{5,21},{6,22},{7,23},{8,56},{9,... | collective-permute-start | bytes 2506760 | tf_op jit(solution)/shard_map/ppermute | solution.py:60
  10.8 20.4 %collective-permute-start.1 = (bf16[544,768]{1,0:T(8,128)(2,1)}, bf16[544,768]{1,0:T(8,128)(2,1)S(1)}, u32[]{:S(2)}, u32[]{:S(2)}) collective-permute-start(bf16[544,768]{1,0:T(8,128)(2,1)} %stage.1.refs_0_.refs_4_), channel_id=1, source_target_pairs={{0,48},{1,49},{2,50},{3,51},{4,52},{5,53},{6,54},{7,55},{8,24},{9,... | collective-permute-start | bytes 2506760 | tf_op jit(solution)/shard_map/ppermute | solution.py:60
  10.8 9.4 %collective-permute-start.3 = (bf16[512,384]{1,0:T(8,128)(2,1)S(1)}, bf16[512,384]{1,0:T(8,128)(2,1)S(1)}, u32[]{:S(2)}, u32[]{:S(2)}) collective-permute-start(bf16[512,384]{1,0:T(8,128)(2,1)S(1)} %copy-done.5), channel_id=1, source_target_pairs={{0,64},{1,65},{2,66},{3,67},{4,68},{5,69},{6,70},{7,71},{8,72},{9,... | collective-permute-start | bytes 1179656 | tf_op jit(solution)/shard_map/ppermute | solution.py:60
  12.7 10.4 %collective-permute-start.4 = (bf16[128,1536]{1,0:T(8,128)(2,1)S(1)}, bf16[128,1536]{1,0:T(8,128)(2,1)S(1)}, u32[]{:S(2)}, u32[]{:S(2)}) collective-permute-start(bf16[128,1536]{1,0:T(8,128)(2,1)S(1)} %lend.1), channel_id=1, source_target_pairs={{0,68},{1,69},{2,70},{3,71},{4,64},{5,65},{6,66},{7,67},{8,76},{9,... | collective-permute-start | bytes 1179656 | tf_op jit(solution)/shard_map/ppermute | solution.py:60
  31.2 4.8 %collective-permute-start.6 = (bf16[544,768]{1,0:T(8,128)(2,1)S(1)}, bf16[544,768]{1,0:T(8,128)(2,1)S(1)}, u32[]{:S(2)}, u32[]{:S(2)}) collective-permute-start(bf16[544,768]{1,0:T(8,128)(2,1)S(1)} %collective-permute-done.refs_0_.refs_1_.refs_5_), channel_id=1, source_target_pairs={{0,8},{1,9},{2,10},{3,11},{4,12},{5,13},{6,14},{7,15},{8,0},{9,1},... | collective-permute-start | bytes 2506760 | tf_op jit(solution)/shard_map/ppermute | solution.py:60
  31.2 6.8 %collective-permute-start.7 = (bf16[544,768]{1,0:T(8,128)(2,1)S(1)}, bf16[544,768]{1,0:T(8,128)(2,1)S(1)}, u32[]{:S(2)}, u32[]{:S(2)}) collective-permute-start(bf16[544,768]{1,0:T(8,128)(2,1)S(1)} %collective-permute-done.1.refs_1_.refs_2_.refs_6_), channel_id=1, source_target_pairs={{0,8},{1,9},{2,10},{3,11},{4,12},{5,13},{6,14},{7,15},{8,0},{9,1},... | collective-permute-start | bytes 2506760 | tf_op jit(solution)/shard_map/ppermute | solution.py:60
  31.7 14.5 %collective-permute-start.5 = (bf16[544,768]{1,0:T(8,128)(2,1)S(1)}, bf16[544,768]{1,0:T(8,128)(2,1)S(1)}, u32[]{:S(2)}, u32[]{:S(2)}) collective-permute-start(bf16[544,768]{1,0:T(8,128)(2,1)S(1)} %collective-permute-done.refs_0_.refs_1_.refs_5_), channel_id=1, source_target_pairs={{0,16},{1,17},{2,18},{3,19},{4,20},{5,21},{6,22},{7,23},{8,56},{9,... | collective-permute-start | bytes 2506760 | tf_op jit(solution)/shard_map/ppermute | solution.py:60
  33.8 12.3 %collective-permute-start.10 = (bf16[256,384]{1,0:T(8,128)(2,1)S(1)}, bf16[256,384]{1,0:T(8,128)(2,1)S(1)}, u32[]{:S(2)}, u32[]{:S(2)}) collective-permute-start(bf16[256,384]{1,0:T(8,128)(2,1)S(1)} %get-tuple-element.78), channel_id=1, source_target_pairs={{0,3},{1,0},{2,1},{3,2},{4,7},{5,4},{6,5},{7,6},{8,9},{9,10},{10,1... | collective-permute-start | bytes 589832 | tf_op jit(solution)/shard_map/ppermute | solution.py:60
  34.3 11.9 %collective-permute-start.11 = (bf16[256,384]{1,0:T(8,128)(2,1)S(1)}, bf16[256,384]{1,0:T(8,128)(2,1)S(1)}, u32[]{:S(2)}, u32[]{:S(2)}) collective-permute-start(bf16[256,384]{1,0:T(8,128)(2,1)S(1)} %get-tuple-element.79), channel_id=1, source_target_pairs={{0,2},{1,3},{2,0},{3,1},{4,6},{5,7},{6,4},{7,5},{8,10},{9,11},{10,... | collective-permute-start | bytes 589832 | tf_op jit(solution)/shard_map/ppermute | solution.py:60
  36.1 10.1 %collective-permute-start.9 = (bf16[256,384]{1,0:T(8,128)(2,1)S(1)}, bf16[256,384]{1,0:T(8,128)(2,1)S(1)}, u32[]{:S(2)}, u32[]{:S(2)}) collective-permute-start(bf16[256,384]{1,0:T(8,128)(2,1)S(1)} %get-tuple-element.77), channel_id=1, source_target_pairs={{0,1},{1,2},{2,3},{3,0},{4,5},{5,6},{6,7},{7,4},{8,11},{9,8},{10,9... | collective-permute-start | bytes 589832 | tf_op jit(solution)/shard_map/ppermute | solution.py:60
  46.2 4.0 %collective-permute-start.12 = (bf16[544,768]{1,0:T(8,128)(2,1)S(1)}, bf16[544,768]{1,0:T(8,128)(2,1)S(1)}, u32[]{:S(2)}, u32[]{:S(2)}) collective-permute-start(bf16[544,768]{1,0:T(8,128)(2,1)S(1)} %collective-permute-done.5.refs_0_.refs_3_.refs_7_), channel_id=1, source_target_pairs={{0,8},{1,9},{2,10},{3,11},{4,12},{5,13},{6,14},{7,15},{8,0},{9,1},... | collective-permute-start | bytes 2506760 | tf_op jit(solution)/shard_map/ppermute | solution.py:60
  47.3 1.7 %copy-start.1 = (bf16[384,3072]{1,0:T(8,128)(2,1)S(1)}, bf16[384,3072]{1,0:T(8,128)(2,1)}, u32[]{:S(2)}) copy-start(bf16[384,3072]{1,0:T(8,128)(2,1)} %w.1) | copy-start | bytes 7077892
  47.3 7.1 %collective-permute-start.14 = (bf16[128,768]{1,0:T(8,128)(2,1)S(1)}, bf16[128,768]{1,0:T(8,128)(2,1)S(1)}, u32[]{:S(2)}, u32[]{:S(2)}) collective-permute-start(bf16[128,768]{1,0:T(8,128)(2,1)S(1)} %prompt.1), channel_id=1, source_target_pairs={{0,64},{1,65},{2,66},{3,67},{4,68},{5,69},{6,70},{7,71},{8,72},{9,... | collective-permute-start | bytes 589832 | tf_op jit(solution)/shard_map/ppermute | solution.py:60
  49.8 19.5 %collective-permute-start.23 = (bf16[384,1536]{1,0:T(8,128)(2,1)S(1)}, bf16[384,1536]{1,0:T(8,128)(2,1)S(1)}, u32[]{:S(2)}, u32[]{:S(2)}) collective-permute-start(bf16[384,1536]{1,0:T(8,128)(2,1)S(1)} %get-tuple-element.110), channel_id=1, source_target_pairs={{0,8},{1,9},{2,10},{3,11},{4,12},{5,13},{6,14},{7,15},{8,0},{9,1},... | collective-permute-start | bytes 3538952 | tf_op jit(solution)/shard_map/ppermute | solution.py:60
  50.0 25.8 %collective-permute-start.24 = (bf16[384,1536]{1,0:T(8,128)(2,1)S(1)}, bf16[384,1536]{1,0:T(8,128)(2,1)S(1)}, u32[]{:S(2)}, u32[]{:S(2)}) collective-permute-start(bf16[384,1536]{1,0:T(8,128)(2,1)S(1)} %get-tuple-element.109.refs_9_), channel_id=1, source_target_pairs={{0,1},{1,2},{2,3},{3,0},{4,5},{5,6},{6,7},{7,4},{8,11},{9,8},{10,9... | collective-permute-start | bytes 3538952 | tf_op jit(solution)/shard_map/ppermute | solution.py:60
  53.0 4.6 %copy-start.6 = (s32[4]{0:T(128)S(1)}, s32[4]{0:T(128)}, u32[]{:S(2)}) copy-start(s32[4]{0:T(128)} %start_ref.1) | copy-start | bytes 52
  53.0 4.6 %copy-start.7 = (s32[4]{0:T(128)S(1)}, s32[4]{0:T(128)}, u32[]{:S(2)}) copy-start(s32[4]{0:T(128)} %length_ref.1) | copy-start | bytes 52
  53.0 11.2 %collective-permute-start.13 = (bf16[544,384]{1,0:T(8,128)(2,1)S(1)}, bf16[544,384]{1,0:T(8,128)(2,1)S(1)}, u32[]{:S(2)}, u32[]{:S(2)}) collective-permute-start(bf16[544,384]{1,0:T(8,128)(2,1)S(1)} %far_other.1), channel_id=1, source_target_pairs={{0,64},{1,65},{2,66},{3,67},{4,68},{5,69},{6,70},{7,71},{8,72},{9,... | collective-permute-start | bytes 1253384 | tf_op jit(solution)/shard_map/ppermute | solution.py:60
  54.4 3.2 %collective-permute-start.15 = (bf16[128,768]{1,0:T(8,128)(2,1)S(1)}, bf16[128,768]{1,0:T(8,128)(2,1)S(1)}, u32[]{:S(2)}, u32[]{:S(2)}) collective-permute-start(bf16[128,768]{1,0:T(8,128)(2,1)S(1)} %collective-permute-done.14.refs_12_), channel_id=1, source_target_pairs={{0,8},{1,9},{2,10},{3,11},{4,12},{5,13},{6,14},{7,15},{8,0},{9,1},... | collective-permute-start | bytes 589832 | tf_op jit(solution)/shard_map/ppermute | solution.py:60
  65.5 4.9 %collective-permute-start.16 = (bf16[128,384]{1,0:T(8,128)(2,1)S(1)}, bf16[128,384]{1,0:T(8,128)(2,1)S(1)}, u32[]{:S(2)}, u32[]{:S(2)}) collective-permute-start(bf16[128,384]{1,0:T(8,128)(2,1)S(1)} %get-tuple-element.106), channel_id=1, source_target_pairs={{0,1},{1,2},{2,3},{3,0},{4,5},{5,6},{6,7},{7,4},{8,11},{9,8},{10,9... | collective-permute-start | bytes 294920 | tf_op jit(solution)/shard_map/ppermute | solution.py:60
  65.5 6.8 %collective-permute-start.17 = (bf16[128,384]{1,0:T(8,128)(2,1)S(1)}, bf16[128,384]{1,0:T(8,128)(2,1)S(1)}, u32[]{:S(2)}, u32[]{:S(2)}) collective-permute-start(bf16[128,384]{1,0:T(8,128)(2,1)S(1)} %get-tuple-element.107), channel_id=1, source_target_pairs={{0,3},{1,0},{2,1},{3,2},{4,7},{5,4},{6,5},{7,6},{8,9},{9,10},{10,1... | collective-permute-start | bytes 294920 | tf_op jit(solution)/shard_map/ppermute | solution.py:60
  67.6 5.8 %collective-permute-start.18 = (bf16[128,384]{1,0:T(8,128)(2,1)S(1)}, bf16[128,384]{1,0:T(8,128)(2,1)S(1)}, u32[]{:S(2)}, u32[]{:S(2)}) collective-permute-start(bf16[128,384]{1,0:T(8,128)(2,1)S(1)} %get-tuple-element.108), channel_id=1, source_target_pairs={{0,2},{1,3},{2,0},{3,1},{4,6},{5,7},{6,4},{7,5},{8,10},{9,11},{10,... | collective-permute-start | bytes 294920 | tf_op jit(solution)/shard_map/ppermute | solution.py:60
  69.3 6.6 %collective-permute-start.19 = (bf16[128,384]{1,0:T(8,128)(2,1)S(1)}, bf16[128,384]{1,0:T(8,128)(2,1)S(1)}, u32[]{:S(2)}, u32[]{:S(2)}) collective-permute-start(bf16[128,384]{1,0:T(8,128)(2,1)S(1)} %get-tuple-element.105.refs_0_), channel_id=1, source_target_pairs={{0,8},{1,9},{2,10},{3,11},{4,12},{5,13},{6,14},{7,15},{8,0},{9,1},... | collective-permute-start | bytes 294920 | tf_op jit(solution)/shard_map/ppermute | solution.py:60
  70.3 5.5 %collective-permute-start.20 = (bf16[128,384]{1,0:T(8,128)(2,1)S(1)}, bf16[128,384]{1,0:T(8,128)(2,1)S(1)}, u32[]{:S(2)}, u32[]{:S(2)}) collective-permute-start(bf16[128,384]{1,0:T(8,128)(2,1)S(1)} %collective-permute-done.16.refs_1_), channel_id=1, source_target_pairs={{0,8},{1,9},{2,10},{3,11},{4,12},{5,13},{6,14},{7,15},{8,0},{9,1},... | collective-permute-start | bytes 294920 | tf_op jit(solution)/shard_map/ppermute | solution.py:60
  72.3 3.5 %collective-permute-start.21 = (bf16[128,384]{1,0:T(8,128)(2,1)S(1)}, bf16[128,384]{1,0:T(8,128)(2,1)S(1)}, u32[]{:S(2)}, u32[]{:S(2)}) collective-permute-start(bf16[128,384]{1,0:T(8,128)(2,1)S(1)} %collective-permute-done.17.refs_2_), channel_id=1, source_target_pairs={{0,8},{1,9},{2,10},{3,11},{4,12},{5,13},{6,14},{7,15},{8,0},{9,1},... | collective-permute-start | bytes 294920 | tf_op jit(solution)/shard_map/ppermute | solution.py:60
  73.3 3.5 %collective-permute-start.22 = (bf16[128,384]{1,0:T(8,128)(2,1)S(1)}, bf16[128,384]{1,0:T(8,128)(2,1)S(1)}, u32[]{:S(2)}, u32[]{:S(2)}) collective-permute-start(bf16[128,384]{1,0:T(8,128)(2,1)S(1)} %collective-permute-done.18.refs_3_), channel_id=1, source_target_pairs={{0,8},{1,9},{2,10},{3,11},{4,12},{5,13},{6,14},{7,15},{8,0},{9,1},... | collective-permute-start | bytes 294920 | tf_op jit(solution)/shard_map/ppermute | solution.py:60
  78.6 7.7 %collective-permute-start.25 = (bf16[64,1536]{1,0:T(8,128)(2,1)S(1)}, bf16[64,1536]{1,0:T(8,128)(2,1)S(1)}, u32[]{:S(2)}, u32[]{:S(2)}) collective-permute-start(bf16[64,1536]{1,0:T(8,128)(2,1)S(1)} %get-tuple-element.112), channel_id=1, source_target_pairs={{0,4},{1,5},{2,6},{3,7},{4,0},{5,1},{6,2},{7,3},{8,12},{9,13},{10,... | collective-permute-start | bytes 589832 | tf_op jit(solution)/shard_map/ppermute | solution.py:60
  81.5 4.8 %collective-permute-start.26 = (bf16[64,1536]{1,0:T(8,128)(2,1)S(1)}, bf16[64,1536]{1,0:T(8,128)(2,1)S(1)}, u32[]{:S(2)}, u32[]{:S(2)}) collective-permute-start(bf16[64,1536]{1,0:T(8,128)(2,1)S(1)} %get-tuple-element.113), channel_id=1, source_target_pairs={{0,8},{1,9},{2,10},{3,11},{4,12},{5,13},{6,14},{7,15},{8,0},{9,1},... | collective-permute-start | bytes 589832 | tf_op jit(solution)/shard_map/ppermute | solution.py:60
  82.2 8.8 %collective-permute-start.27 = (bf16[64,1536]{1,0:T(8,128)(2,1)S(1)}, bf16[64,1536]{1,0:T(8,128)(2,1)S(1)}, u32[]{:S(2)}, u32[]{:S(2)}) collective-permute-start(bf16[64,1536]{1,0:T(8,128)(2,1)S(1)} %get-tuple-element.114), channel_id=1, source_target_pairs={{0,12},{1,13},{2,14},{3,15},{4,8},{5,9},{6,10},{7,11},{8,4},{9,5},... | collective-permute-start | bytes 589832 | tf_op jit(solution)/shard_map/ppermute | solution.py:60

commit v3 on v2

--- a/solution.py
+++ b/solution.py
@@ -32,7 +32,7 @@
     return pl.CostEstimate(flops=int(us * 1.15e9), bytes_accessed=1024, transcendentals=0)
 
 
-TIMES = dict(near_mine=2.4, near_other=2.4, mid=8.0, far_other=2.8, far_mine=26.0, side=20.0, join=20.0)
+TIMES = dict(near_mine=2.4, near_other=2.4, mid=8.0, far_other=2.8, far_mine=26.0, side=2.7, join=20.0)
 SMEM = pl.BlockSpec(memory_space=pltpu.SMEM)
 VMEM = pl.BlockSpec(memory_space=pltpu.VMEM)
 HBM = pl.BlockSpec(memory_space=pltpu.HBM)
@@ -123,20 +123,17 @@
     )(here, w, came)
 
 
-def lend_body(here, ak, av, out, sem):
-    width = out.shape[1]
-    rows = ak.shape[0]
-    cols = pl.ds(pl.multiple_of((1 - here[3]) * width, width), width)
-    move(sem, (ak.at[:, cols], out.at[pl.ds(0, rows)]), (av.at[:, cols], out.at[pl.ds(rows, rows)]))
+def lend_body(here, ak, av, out):
+    cols = pl.ds(pl.multiple_of((1 - here[3]) * out.shape[1], out.shape[1]), out.shape[1])
+    out[...] = jnp.where(here[0] == 0, ak[:, cols], av[:, cols])
 
 
 def lend(here, ak, av):
     return pl.pallas_call(
         lend_body,
-        out_shape=jax.ShapeDtypeStruct((2 * ak.shape[0], ak.shape[1] // 2), BF16),
-        in_specs=[SMEM, HBM, HBM],
+        out_shape=jax.ShapeDtypeStruct((ak.shape[0], ak.shape[1] // 2), BF16),
+        in_specs=[SMEM, VMEM, VMEM],
         out_specs=VMEM,
-        scratch_shapes=[pltpu.SemaphoreType.DMA((2,))],
         compiler_params=PARAMS,
         cost_estimate=COST,
         name="lend",
@@ -171,15 +168,14 @@
     for out, shift in zip(outs, (0, step, -step, 2)):
         target = lax.rem(z + shift + 4, 4)
         cols = pl.ds(pl.multiple_of((y_hi * 4 + target) * GROUP, GROUP), GROUP)
-        out[:rows, :] = ak[:, cols]
-        out[rows : 2 * rows, :] = av[:, cols]
-        out[2 * rows :, :] = lent[:, pl.ds(pl.multiple_of(target * GROUP, GROUP), GROUP)]
+        out[:rows, :] = jnp.where(core == 0, ak[:, cols], av[:, cols])
+        out[rows:, :] = lent[:, pl.ds(pl.multiple_of(target * GROUP, GROUP), GROUP)]
 
 
 def deal(here, ak, av, lent):
     return pl.pallas_call(
         deal_body,
-        out_shape=[jax.ShapeDtypeStruct((4 * ak.shape[0], GROUP), BF16)] * 4,
+        out_shape=[jax.ShapeDtypeStruct((2 * ak.shape[0], GROUP), BF16)] * 4,
         in_specs=[SMEM, VMEM, VMEM, VMEM],
         out_specs=[VMEM] * 4,
         compiler_params=PARAMS,
@@ -280,7 +276,7 @@
 
 
 def side_body(here, start_ref, length_ref, prompt_ref, q_ref, *refs):
-    audios, texts, out_ref = refs[:4], refs[4:14], refs[14]
+    mine, theirs, texts, out_ref = refs[:4], refs[4:8], refs[8:18], refs[18]
     core, x, y_lo, y_hi, z = [here[i] for i in range(5)]
     lane = lax.broadcasted_iota(jnp.int32, (1, 16 * TEXT), 1)
     place = jnp.zeros((1, 16 * TEXT), jnp.int32)
@@ -292,12 +288,11 @@
         block = y * 8 + lax.rem(x + shift + 4, 4) * 2 + c
         place = jnp.where(lane // TEXT == number, block * TEXT + lane % TEXT, place)
     live = place < prompt_ref[0]
-    shard = audios[0].shape[0] // 4
+    shard = mine[0].shape[0] // 2
     heard_at = jnp.zeros((1, 8 * shard), jnp.int32)
     lane = lax.broadcasted_iota(jnp.int32, (1, 8 * shard), 1)
-    step = 1 - 2 * core
     for number in range(8):
-        source = lax.rem(z + (0, -step, step, 2)[number // 2] + 4, 4)
+        source = lax.rem(z + (0, 3, 1, 2)[number // 2], 4)
         y = y_hi if number % 2 == 0 else 1 - y_hi
         block = y * 4 + source
         heard_at = jnp.where(lane // shard == number, block * shard + lane % shard, heard_at)
@@ -306,10 +301,10 @@
         vcols = pl.ds(GROUP + head * HD, HD)
         text_k = jnp.concatenate([ref[:, cols] for ref in texts], axis=0)
         text_v = with_ones(jnp.concatenate([ref[:, vcols] for ref in texts], axis=0))
-        parts = [(ref, half) for ref in audios for half in (0, 2 * shard)]
-        audio_k = jnp.concatenate([ref[pl.ds(half, shard), cols] for ref, half in parts], axis=0)
-        audio_v = [ref[pl.ds(half + shard, shard), cols] for ref, half in parts]
-        audio_v = with_ones(jnp.concatenate(audio_v, axis=0))
+        pick = lambda refs, order: jnp.concatenate([refs[i][:, cols] for i in order], axis=0)
+        first, second = (0, 1, 2, 3), (0, 2, 1, 3)
+        audio_k = jnp.where(core == 0, pick(mine, first), pick(theirs, first))
+        audio_v = with_ones(jnp.where(core == 0, pick(theirs, second), pick(mine, second)))
         for block in range(ROWS // HD):
             rows = pl.ds(block * HD, HD)
             q = q_ref[rows, cols]
@@ -331,7 +326,7 @@
         side_body,
         out_shape=jax.ShapeDtypeStruct(q.shape, F32),
         grid=(1,),
-        in_specs=[SMEM] * 4 + [VMEM] * 5 + [BELOW] * 8 + [VMEM] * 2,
+        in_specs=[SMEM] * 4 + [VMEM] * 9 + [BELOW] * 8 + [VMEM] * 2,
         out_specs=VMEM,
         compiler_params=PARAMS,
         cost_estimate=lasting(TIMES["side"]),
@@ -469,17 +464,18 @@
     kv1_c = send(kv1, CORE)
     kv2_c = send(kv2, CORE)
     mid_mine, mid_other = flash("mid", [kv1, kv2, kv1_c, kv2_c], [after(video_q, came), asked])
-    kv3, mid_mine, mid_other, *audios = lax.optimization_barrier(
-        (kv3, mid_mine, mid_other, *audios)
-    )
-    kv3_c = send(kv3, CORE)
     w0, w1, w2 = split(here, w_out, after(came, *mid_mine))
+    kv3, mid_mine, mid_other, w0, *audios = lax.optimization_barrier(
+        (kv3, mid_mine, mid_other, w0, *audios)
+    )
     w3 = send(w1, Z_A)
     w2 = send(w2, CORE)
+    audios += [send(audio, CORE) for audio in audios]
+    kv3_c = send(kv3, CORE)
     text = prompt(own, kv1, kv2, kv3)
     text_y = send(text, Y_LO)
     (packed,) = flash(
-        "far_other", [kv3, kv3_c], [after(asked, w0)], [[near_other, mid_other]], packed=True
+        "far_other", [kv3, kv3_c], [after(asked, *audios)], [[near_other, mid_other]], packed=True
     )
     got = send(packed, Y_LO)
     text_y = after(text_y, packed)

time: 92.6 us -> 93.6 us (1.011)
    ppermute x28 -> x32, starting transfers between devices: 34.3 us -> 34.5 us  [send(): return lax.ppermute(array, AXES, route)]
    ppermute x28 -> x32, waiting for transfers between devices: 25.9 us -> 26.1 us  [send(): return lax.ppermute(array, AXES, route)]
  transfers between devices with their start and end apart: 28 -> 32, of which waited for: 9 -> 10; matrix products, arithmetic and copies ran while one was open for 1% -> 1% of each run, Pallas kernels for 30% -> 29%
where the time goes in v3:
time: 93.6 us; the launch traced here: 93.4 us
  starting transfers between devices  34.5 us (37%)
  Pallas kernels  30.1 us (32%)
  waiting for transfers between devices  26.1 us (28%)
  local copies, waits for them, and re-layouts  1.75 us (2%)
    ppermute x32, starting transfers between devices, send(): return lax.ppermute(array, AXES, route)  34.5 us
    ppermute x32, waiting for transfers between devices, send(): return lax.ppermute(array, AXES, route)  26.1 us
    pallas_call x5, Pallas kernels, flash(): pl.pallas_call(functools.partial(flash_body, n_arrays, n_sets, n_priors,...  18 us
    pallas_call x1, Pallas kernels, stage(): pl.pallas_call(stage_body, out_shape=jax.ShapeDtypeStruct((ROWS + TEXT, 2...  2.85 us
    pallas_call x1, Pallas kernels, side(): pl.pallas_call(side_body, out_shape=jax.ShapeDtypeStruct(q.shape, F32), g...  2.76 us
  transfers between devices with their start and end apart: 32, of which 10 were waited for; matrix products, arithmetic and copies ran while one was open for 1% of the time, Pallas kernels for 29%

profile of v3, /device:TPU:1, one launch (start us, length us, event | category | flops | bytes accessed | tf_op | source)
XLA Modules:
  0.0 93.4 jit_solution(5784608202351402073)
XLA Ops:
  0.0 4.7 %collective-permute-start.8 = (bf16[384,3072]{1,0:T(8,128)(2,1)}, bf16[384,3072]{1,0:T(8,128)(2,1)S(1)}, u32[]{:S(2)}, u32[]{:S(2)}) collective-permute-start(bf16[384,3072]{1,0:T(8,128)(2,1)} %w.1), channel_id=1, source_target_pairs={{0,1},{1,2},{2,3},{3,0},{4,5},{5,6},{6,7},{7,4},{8,11},{9,8},{10,9... | collective-permute-start | bytes 7077896 | tf_op jit(solution)/shard_map/ppermute | solution.py:60
  4.7 0.6 stack.23._.here
  5.2 2.9 %stage.1.refs_0_.refs_8_ = bf16[544,768]{1,0:T(8,128)(2,1)} custom-call(s32[5]{0:T(128)} %stack.23._.here, bf16[512,384]{1,0:T(8,128)(2,1)} %k.1, bf16[512,384]{1,0:T(8,128)(2,1)} %v.1, bf16[32,384]{1,0:T(8,128)(2,1)} %tk.1, bf16[32,384]{1,0:T(8,128)(2,1)} %tv.1), custom_call_target="tpu_custom_call" | custom-call | flops 1024 | bytes 1024 | tf_op jit(solution)/shard_map/stage/pallas_call | solution.py:92
  8.2 2.5 %collective-permute-start = (bf16[544,768]{1,0:T(8,128)(2,1)}, bf16[544,768]{1,0:T(8,128)(2,1)S(1)}, u32[]{:S(2)}, u32[]{:S(2)}) collective-permute-start(bf16[544,768]{1,0:T(8,128)(2,1)} %stage.1.refs_0_.refs_8_), channel_id=1, source_target_pairs={{0,16},{1,17},{2,18},{3,19},{4,20},{5,21},{6,22},{7,23},{8,56},{9,... | collective-permute-start | bytes 2506760 | tf_op jit(solution)/shard_map/ppermute | solution.py:60
  10.7 1.3 %collective-permute-start.3 = (bf16[512,384]{1,0:T(8,128)(2,1)S(1)}, bf16[512,384]{1,0:T(8,128)(2,1)S(1)}, u32[]{:S(2)}, u32[]{:S(2)}) collective-permute-start(bf16[512,384]{1,0:T(8,128)(2,1)S(1)} %copy-done.6), channel_id=1, source_target_pairs={{0,64},{1,65},{2,66},{3,67},{4,68},{5,69},{6,70},{7,71},{8,72},{9,... | collective-permute-start | bytes 1179656 | tf_op jit(solution)/shard_map/ppermute | solution.py:60
  12.0 0.6 lend.1
  12.6 2.0 %collective-permute-start.4 = (bf16[64,1536]{1,0:T(8,128)(2,1)S(1)}, bf16[64,1536]{1,0:T(8,128)(2,1)S(1)}, u32[]{:S(2)}, u32[]{:S(2)}) collective-permute-start(bf16[64,1536]{1,0:T(8,128)(2,1)S(1)} %lend.1), channel_id=1, source_target_pairs={{0,68},{1,69},{2,70},{3,71},{4,64},{5,65},{6,66},{7,67},{8,76},{9,... | collective-permute-start | bytes 589832 | tf_op jit(solution)/shard_map/ppermute | solution.py:60
  14.6 1.1 %copy-done = bf16[544,768]{1,0:T(8,128)(2,1)S(1)} copy-done((bf16[544,768]{1,0:T(8,128)(2,1)S(1)}, bf16[544,768]{1,0:T(8,128)(2,1)}, u32[]{:S(2)}) %copy-start) | copy-done | bytes 835608
  15.8 2.3 %near_mine.1 = (f32[512,384]{1,0:T(8,128)S(1)}, f32[512,384]{1,0:T(8,128)S(1)}, f32[512,384]{1,0:T(8,128)S(1)}) custom-call(bf16[544,768]{1,0:T(8,128)(2,1)S(1)} %copy-done, bf16[544,768]{1,0:T(8,128)(2,1)S(1)} %collective-permute-done.2.refs_1_.refs_12_, bf16[512,384]{1,0:T(8,128)(2,1)S(1)} %copy-done.6), custom_call_target="tpu_custom_call" | custom-call | flops 2760000000 | bytes 1024 | tf_op jit(solution)/shard_map/near_mine/pallas_call | solution.py:268
  18.1 2.1 %collective-permute-done.3.refs_2_.refs_5_ = bf16[512,384]{1,0:T(8,128)(2,1)S(1)} collective-permute-done((bf16[512,384]{1,0:T(8,128)(2,1)S(1)}, bf16[512,384]{1,0:T(8,128)(2,1)S(1)}, u32[]{:S(2)}, u32[]{:S(2)}) %collective-permute-start.3) | collective-permute-done | bytes 393248 | tf_op jit(solution)/shard_map/ppermute | solution.py:60
  20.2 2.3 %near_other.1 = (f32[512,384]{1,0:T(8,128)S(1)}, f32[512,384]{1,0:T(8,128)S(1)}, f32[512,384]{1,0:T(8,128)S(1)}) custom-call(bf16[544,768]{1,0:T(8,128)(2,1)S(1)} %copy-done, bf16[544,768]{1,0:T(8,128)(2,1)S(1)} %collective-permute-done.2.refs_1_.refs_12_, bf16[512,384]{1,0:T(8,128)(2,1)S(1)} %collective-permute-done.3.refs_2_.refs_5_), custom_call_target="tpu_custom_call" | custom-call | flops 2760000000 | bytes 1024 | tf_op jit(solution)/shard_map/near_other/pallas_call | solution.py:268
  22.5 5.5 %collective-permute-done.refs_0_.refs_1_.refs_9_ = bf16[544,768]{1,0:T(8,128)(2,1)S(1)} collective-permute-done((bf16[544,768]{1,0:T(8,128)(2,1)}, bf16[544,768]{1,0:T(8,128)(2,1)S(1)}, u32[]{:S(2)}, u32[]{:S(2)}) %collective-permute-start) | collective-permute-done | bytes 835616 | tf_op jit(solution)/shard_map/ppermute | solution.py:60
  28.0 3.1 %collective-permute-done.1.refs_1_.refs_2_.refs_10_ = bf16[544,768]{1,0:T(8,128)(2,1)S(1)} collective-permute-done((bf16[544,768]{1,0:T(8,128)(2,1)}, bf16[544,768]{1,0:T(8,128)(2,1)S(1)}, u32[]{:S(2)}, u32[]{:S(2)}) %collective-permute-start.1) | collective-permute-done | bytes 835616 | tf_op jit(solution)/shard_map/ppermute | solution.py:60
  31.2 0.5 collective-permute-start.7
  31.7 1.5 %collective-permute-start.5 = (bf16[544,768]{1,0:T(8,128)(2,1)S(1)}, bf16[544,768]{1,0:T(8,128)(2,1)S(1)}, u32[]{:S(2)}, u32[]{:S(2)}) collective-permute-start(bf16[544,768]{1,0:T(8,128)(2,1)S(1)} %collective-permute-done.refs_0_.refs_1_.refs_9_), channel_id=1, source_target_pairs={{0,16},{1,17},{2,18},{3,19},{4,20},{5,21},{6,22},{7,23},{8,56},{9,... | collective-permute-start | bytes 2506760 | tf_op jit(solution)/shard_map/ppermute | solution.py:60
  33.2 0.6 deal.1
  33.8 0.5 collective-permute-start.10
  34.2 1.8 %collective-permute-start.11 = (bf16[128,384]{1,0:T(8,128)(2,1)S(1)}, bf16[128,384]{1,0:T(8,128)(2,1)S(1)}, u32[]{:S(2)}, u32[]{:S(2)}) collective-permute-start(bf16[128,384]{1,0:T(8,128)(2,1)S(1)} %get-tuple-element.82), channel_id=1, source_target_pairs={{0,2},{1,3},{2,0},{3,1},{4,6},{5,7},{6,4},{7,5},{8,10},{9,11},{10,... | collective-permute-start | bytes 294920 | tf_op jit(solution)/shard_map/ppermute | solution.py:60
  36.0 2.0 %collective-permute-start.9 = (bf16[128,384]{1,0:T(8,128)(2,1)S(1)}, bf16[128,384]{1,0:T(8,128)(2,1)S(1)}, u32[]{:S(2)}, u32[]{:S(2)}) collective-permute-start(bf16[128,384]{1,0:T(8,128)(2,1)S(1)} %get-tuple-element.80), channel_id=1, source_target_pairs={{0,1},{1,2},{2,3},{3,0},{4,5},{5,6},{6,7},{7,4},{8,11},{9,8},{10,9... | collective-permute-start | bytes 294920 | tf_op jit(solution)/shard_map/ppermute | solution.py:60
  38.0 7.9 %mid.1 = (f32[512,384]{1,0:T(8,128)S(1)}, f32[512,384]{1,0:T(8,128)S(1)}, f32[512,384]{1,0:T(8,128)S(1)}, f32[512,384]{1,0:T(8,128)S(1)}, f32[512,384]{1,0:T(8,128)S(1)}, /*index=5*/f32[512,384]{1,0:T(8,128)S(1)}) custom-call(bf16[544,768]{1,0:T(8,128)(2,1)S(1)} %collective-permute-done.refs_0_.refs_1_.refs_9_, ...), custom_call_target="tpu_custom_call" | custom-call | flops 9200000000 | bytes 1024 | tf_op jit(solution)/shard_map/mid/pallas_call | solution.py:268
  46.0 0.8 split.1
  46.9 0.5 collective-permute-start.13
  47.5 0.4 collective-permute-start.15
  48.7 0.7 collective-permute-done.13.refs_4_
  49.4 1.3 %collective-permute-start.18 = (bf16[128,768]{1,0:T(8,128)(2,1)S(1)}, bf16[128,768]{1,0:T(8,128)(2,1)S(1)}, u32[]{:S(2)}, u32[]{:S(2)}) collective-permute-start(bf16[128,768]{1,0:T(8,128)(2,1)S(1)} %prompt.1), channel_id=1, source_target_pairs={{0,64},{1,65},{2,66},{3,67},{4,68},{5,69},{6,70},{7,71},{8,72},{9,... | collective-permute-start | bytes 589832 | tf_op jit(solution)/shard_map/ppermute | solution.py:60
  50.7 0.4 collective-permute-start.27
  51.1 2.8 %far_other.1 = bf16[544,384]{1,0:T(8,128)(2,1)S(1)} custom-call(bf16[544,768]{1,0:T(8,128)(2,1)S(1)} %collective-permute-done.5.refs_0_.refs_3_.refs_11_, bf16[544,768]{1,0:T(8,128)(2,1)S(1)} %collective-permute-done.12.refs_1_.refs_15_, bf16[512,384]{1,0:T(8,128)(2,1)S(1)} %collective-permute-done.3.refs_2_.refs_5_, ...), custom_call_target="tpu_custom_call" | custom-call | flops 3220000000 | bytes 1024 | tf_op jit(solution)/shard_map/far_other/pallas_call | solution.py:268
  54.0 0.2 collective-permute-start.17
  54.2 1.5 %collective-permute-done.18.refs_16_ = bf16[128,768]{1,0:T(8,128)(2,1)S(1)} collective-permute-done((bf16[128,768]{1,0:T(8,128)(2,1)S(1)}, bf16[128,768]{1,0:T(8,128)(2,1)S(1)}, u32[]{:S(2)}, u32[]{:S(2)}) %collective-permute-start.18) | collective-permute-done | bytes 196640 | tf_op jit(solution)/shard_map/ppermute | solution.py:60
  55.7 1.0 %collective-permute-start.19 = (bf16[128,768]{1,0:T(8,128)(2,1)S(1)}, bf16[128,768]{1,0:T(8,128)(2,1)S(1)}, u32[]{:S(2)}, u32[]{:S(2)}) collective-permute-start(bf16[128,768]{1,0:T(8,128)(2,1)S(1)} %collective-permute-done.18.refs_16_), channel_id=1, source_target_pairs={{0,8},{1,9},{2,10},{3,11},{4,12},{5,13},{6,14},{7,15},{8,0},{9,1},... | collective-permute-start | bytes 589832 | tf_op jit(solution)/shard_map/ppermute | solution.py:60
  56.7 2.6 %far_mine.1 = (f32[512,384]{1,0:T(8,128)S(1)}, f32[512,384]{1,0:T(8,128)S(1)}, f32[512,384]{1,0:T(8,128)S(1)}) custom-call(bf16[544,768]{1,0:T(8,128)(2,1)S(1)} %collective-permute-done.5.refs_0_.refs_3_.refs_11_, bf16[544,768]{1,0:T(8,128)(2,1)S(1)} %collective-permute-done.12.refs_1_.refs_15_, bf16[512,384]{1,0:T(8,128)(2,1)S(1)} %copy-done.6, ...), custom_call_target="tpu_custom_call" | custom-call | flops 29899999232 | bytes 1024 | tf_op jit(solution)/shard_map/far_mine/pallas_call | solution.py:268
  59.3 2.8 %side.1.refs_4_ = f32[512,384]{1,0:T(8,128)S(1)} custom-call(s32[5]{0:T(128)S(1)} %copy-done.5, s32[4]{0:T(128)S(1)} %copy-done.7, s32[4]{0:T(128)S(1)} %copy-done.8, s32[1]{0:T(128)S(6)} %copy.12.prompt_ref, bf16[512,384]{1,0:T(8,128)(2,1)S(1)} %copy-done.6, bf16[128,384]{1,0:T(8,128)(2,1)S(1)} %get-tuple-element.84.refs_0_, ...), custom_call_target="tpu_custom_call" | custom-call | flops 3104999936 | bytes 1024 | tf_op jit(solution)/shard_map/side/pallas_call | solution.py:325
  62.1 2.9 %collective-permute-done.17.refs_3_ = bf16[544,384]{1,0:T(8,128)(2,1)S(1)} collective-permute-done((bf16[544,384]{1,0:T(8,128)(2,1)S(1)}, bf16[544,384]{1,0:T(8,128)(2,1)S(1)}, u32[]{:S(2)}, u32[]{:S(2)}) %collective-permute-start.17) | collective-permute-done | bytes 417824 | tf_op jit(solution)/shard_map/ppermute | solution.py:60
  65.0 1.2 %join.1 = (bf16[128,384]{1,0:T(8,128)(2,1)S(1)}, bf16[128,384]{1,0:T(8,128)(2,1)S(1)}, bf16[128,384]{1,0:T(8,128)(2,1)S(1)}, bf16[128,384]{1,0:T(8,128)(2,1)S(1)}) custom-call(s32[5]{0:T(128)S(1)} %copy-done.5, f32[512,384]{1,0:T(8,128)S(1)} %get-tuple-element.102.refs_0_, f32[512,384]{1,0:T(8,128)S(1)} %get-tuple-element.103.refs_1_, ...), custom_call_target="tpu_custom_call" | custom-call | flops 23000000512 | bytes 1024 | tf_op jit(solution)/shard_map/join/pallas_call | solution.py:362
  66.3 2.1 %collective-permute-start.21 = (bf16[128,384]{1,0:T(8,128)(2,1)S(1)}, bf16[128,384]{1,0:T(8,128)(2,1)S(1)}, u32[]{:S(2)}, u32[]{:S(2)}) collective-permute-start(bf16[128,384]{1,0:T(8,128)(2,1)S(1)} %get-tuple-element.108), channel_id=1, source_target_pairs={{0,3},{1,0},{2,1},{3,2},{4,7},{5,4},{6,5},{7,6},{8,9},{9,10},{10,1... | collective-permute-start | bytes 294920 | tf_op jit(solution)/shard_map/ppermute | solution.py:60
  68.4 1.7 %collective-permute-start.22 = (bf16[128,384]{1,0:T(8,128)(2,1)S(1)}, bf16[128,384]{1,0:T(8,128)(2,1)S(1)}, u32[]{:S(2)}, u32[]{:S(2)}) collective-permute-start(bf16[128,384]{1,0:T(8,128)(2,1)S(1)} %get-tuple-element.109), channel_id=1, source_target_pairs={{0,2},{1,3},{2,0},{3,1},{4,6},{5,7},{6,4},{7,5},{8,10},{9,11},{10,... | collective-permute-start | bytes 294920 | tf_op jit(solution)/shard_map/ppermute | solution.py:60
  70.1 1.2 %collective-permute-start.23 = (bf16[128,384]{1,0:T(8,128)(2,1)S(1)}, bf16[128,384]{1,0:T(8,128)(2,1)S(1)}, u32[]{:S(2)}, u32[]{:S(2)}) collective-permute-start(bf16[128,384]{1,0:T(8,128)(2,1)S(1)} %get-tuple-element.106.refs_0_), channel_id=1, source_target_pairs={{0,8},{1,9},{2,10},{3,11},{4,12},{5,13},{6,14},{7,15},{8,0},{9,1},... | collective-permute-start | bytes 294920 | tf_op jit(solution)/shard_map/ppermute | solution.py:60
  71.3 1.9 %collective-permute-start.24 = (bf16[128,384]{1,0:T(8,128)(2,1)S(1)}, bf16[128,384]{1,0:T(8,128)(2,1)S(1)}, u32[]{:S(2)}, u32[]{:S(2)}) collective-permute-start(bf16[128,384]{1,0:T(8,128)(2,1)S(1)} %collective-permute-done.20.refs_1_), channel_id=1, source_target_pairs={{0,8},{1,9},{2,10},{3,11},{4,12},{5,13},{6,14},{7,15},{8,0},{9,1},... | collective-permute-start | bytes 294920 | tf_op jit(solution)/shard_map/ppermute | solution.py:60
  73.3 0.5 collective-permute-start.25
  73.8 0.4 collective-permute-done.22.refs_3_
  74.2 2.6 %collective-permute-start.26 = (bf16[128,384]{1,0:T(8,128)(2,1)S(1)}, bf16[128,384]{1,0:T(8,128)(2,1)S(1)}, u32[]{:S(2)}, u32[]{:S(2)}) collective-permute-start(bf16[128,384]{1,0:T(8,128)(2,1)S(1)} %collective-permute-done.22.refs_3_), channel_id=1, source_target_pairs={{0,8},{1,9},{2,10},{3,11},{4,12},{5,13},{6,14},{7,15},{8,0},{9,1},... | collective-permute-start | bytes 294920 | tf_op jit(solution)/shard_map/ppermute | solution.py:60
  76.8 0.9 collective-permute-done.26.refs_7_
  77.7 1.8 %project.1 = (f32[64,1536]{1,0:T(8,128)S(1)}, bf16[64,1536]{1,0:T(8,128)(2,1)S(1)}, bf16[64,1536]{1,0:T(8,128)(2,1)S(1)}, bf16[64,1536]{1,0:T(8,128)(2,1)S(1)}) custom-call(bf16[128,384]{1,0:T(8,128)(2,1)S(1)} %get-tuple-element.106.refs_0_, bf16[128,384]{1,0:T(8,128)(2,1)S(1)} %collective-permute-done.20.refs_1_, ...), custom_call_target="tpu_custom_call" | custom-call | flops 1024 | bytes 1024 | tf_op jit(solution)/shard_map/project/pallas_call | solution.py:395
  79.5 2.7 %collective-permute-start.29 = (bf16[64,1536]{1,0:T(8,128)(2,1)S(1)}, bf16[64,1536]{1,0:T(8,128)(2,1)S(1)}, u32[]{:S(2)}, u32[]{:S(2)}) collective-permute-start(bf16[64,1536]{1,0:T(8,128)(2,1)S(1)} %get-tuple-element.114), channel_id=1, source_target_pairs={{0,4},{1,5},{2,6},{3,7},{4,0},{5,1},{6,2},{7,3},{8,12},{9,13},{10,... | collective-permute-start | bytes 589832 | tf_op jit(solution)/shard_map/ppermute | solution.py:60
  82.2 0.6 collective-permute-start.30
  83.1 4.2 %collective-permute-done.29.pair = bf16[64,1536]{1,0:T(8,128)(2,1)S(1)} collective-permute-done((bf16[64,1536]{1,0:T(8,128)(2,1)S(1)}, bf16[64,1536]{1,0:T(8,128)(2,1)S(1)}, u32[]{:S(2)}, u32[]{:S(2)}) %collective-permute-start.29) | collective-permute-done | bytes 196640 | tf_op jit(solution)/shard_map/ppermute | solution.py:60
  87.2 4.7 %collective-permute-done.31.both = bf16[64,1536]{1,0:T(8,128)(2,1)S(1)} collective-permute-done((bf16[64,1536]{1,0:T(8,128)(2,1)S(1)}, bf16[64,1536]{1,0:T(8,128)(2,1)S(1)}, u32[]{:S(2)}, u32[]{:S(2)}) %collective-permute-start.31) | collective-permute-done | bytes 196640 | tf_op jit(solution)/shard_map/ppermute | solution.py:60
  91.9 1.4 %total.1 = bf16[64,3072]{1,0:T(8,128)(2,1)} custom-call(s32[5]{0:T(128)S(1)} %copy-done.5, f32[64,1536]{1,0:T(8,128)S(1)} %get-tuple-element.113.keep, bf16[64,1536]{1,0:T(8,128)(2,1)S(1)} %collective-permute-done.29.pair, bf16[64,1536]{1,0:T(8,128)(2,1)S(1)} %collective-permute-done.30.core, bf16[64,1536]{1,0:T(8,128)(2,1)S(1)} %collective-permute-done.31.both), custom_call_target="tpu_custom_call" | custom-call | flops 1024 | bytes 1024 | tf_op jit(solution)/shard_map/total/pallas_call | solution.py:421
  (49 shorter events, 0.8 us)
Async XLA Ops:
  0.0 10.7 %copy-start.6 = (bf16[512,384]{1,0:T(8,128)(2,1)S(1)}, bf16[512,384]{1,0:T(8,128)(2,1)}, u32[]{:S(2)}) copy-start(bf16[512,384]{1,0:T(8,128)(2,1)} %q_ref) | copy-start | bytes 1179652
  0.0 12.0 %copy-start.3 = (bf16[64,3072]{1,0:T(8,128)(2,1)S(1)}, bf16[64,3072]{1,0:T(8,128)(2,1)}, u32[]{:S(2)}) copy-start(bf16[64,3072]{1,0:T(8,128)(2,1)} %ak.3) | copy-start | bytes 1179652
  0.0 12.0 %copy-start.4 = (bf16[64,3072]{1,0:T(8,128)(2,1)S(1)}, bf16[64,3072]{1,0:T(8,128)(2,1)}, u32[]{:S(2)}) copy-start(bf16[64,3072]{1,0:T(8,128)(2,1)} %av.3) | copy-start | bytes 1179652
  0.0 34.2 %collective-permute-start.8 = (bf16[384,3072]{1,0:T(8,128)(2,1)}, bf16[384,3072]{1,0:T(8,128)(2,1)S(1)}, u32[]{:S(2)}, u32[]{:S(2)}) collective-permute-start(bf16[384,3072]{1,0:T(8,128)(2,1)} %w.1), channel_id=1, source_target_pairs={{0,1},{1,2},{2,3},{3,0},{4,5},{5,6},{6,7},{7,4},{8,11},{9,8},{10,9... | collective-permute-start | bytes 7077896 | tf_op jit(solution)/shard_map/ppermute | solution.py:60
  5.2 6.8 %copy-start.5 = (s32[5]{0:T(128)S(1)}, s32[5]{0:T(128)}, u32[]{:S(2)}) copy-start(s32[5]{0:T(128)} %stack.23._.here) | copy-start | bytes 64
  8.1 4.5 %collective-permute-start.2 = (bf16[544,768]{1,0:T(8,128)(2,1)}, bf16[544,768]{1,0:T(8,128)(2,1)S(1)}, u32[]{:S(2)}, u32[]{:S(2)}) collective-permute-start(bf16[544,768]{1,0:T(8,128)(2,1)} %stage.1.refs_0_.refs_8_), channel_id=1, source_target_pairs={{0,8},{1,9},{2,10},{3,11},{4,12},{5,13},{6,14},{7,15},{8,0},{9,1},... | collective-permute-start | bytes 2506760 | tf_op jit(solution)/shard_map/ppermute | solution.py:60
  8.2 19.9 %collective-permute-start = (bf16[544,768]{1,0:T(8,128)(2,1)}, bf16[544,768]{1,0:T(8,128)(2,1)S(1)}, u32[]{:S(2)}, u32[]{:S(2)}) collective-permute-start(bf16[544,768]{1,0:T(8,128)(2,1)} %stage.1.refs_0_.refs_8_), channel_id=1, source_target_pairs={{0,16},{1,17},{2,18},{3,19},{4,20},{5,21},{6,22},{7,23},{8,56},{9,... | collective-permute-start | bytes 2506760 | tf_op jit(solution)/shard_map/ppermute | solution.py:60
  10.7 20.4 %collective-permute-start.1 = (bf16[544,768]{1,0:T(8,128)(2,1)}, bf16[544,768]{1,0:T(8,128)(2,1)S(1)}, u32[]{:S(2)}, u32[]{:S(2)}) collective-permute-start(bf16[544,768]{1,0:T(8,128)(2,1)} %stage.1.refs_0_.refs_8_), channel_id=1, source_target_pairs={{0,48},{1,49},{2,50},{3,51},{4,52},{5,53},{6,54},{7,55},{8,24},{9,... | collective-permute-start | bytes 2506760 | tf_op jit(solution)/shard_map/ppermute | solution.py:60
  10.7 9.4 %collective-permute-start.3 = (bf16[512,384]{1,0:T(8,128)(2,1)S(1)}, bf16[512,384]{1,0:T(8,128)(2,1)S(1)}, u32[]{:S(2)}, u32[]{:S(2)}) collective-permute-start(bf16[512,384]{1,0:T(8,128)(2,1)S(1)} %copy-done.6), channel_id=1, source_target_pairs={{0,64},{1,65},{2,66},{3,67},{4,68},{5,69},{6,70},{7,71},{8,72},{9,... | collective-permute-start | bytes 1179656 | tf_op jit(solution)/shard_map/ppermute | solution.py:60
  12.6 9.9 %collective-permute-start.4 = (bf16[64,1536]{1,0:T(8,128)(2,1)S(1)}, bf16[64,1536]{1,0:T(8,128)(2,1)S(1)}, u32[]{:S(2)}, u32[]{:S(2)}) collective-permute-start(bf16[64,1536]{1,0:T(8,128)(2,1)S(1)} %lend.1), channel_id=1, source_target_pairs={{0,68},{1,69},{2,70},{3,71},{4,64},{5,65},{6,66},{7,67},{8,76},{9,... | collective-permute-start | bytes 589832 | tf_op jit(solution)/shard_map/ppermute | solution.py:60
  14.6 1.1 %copy-start = (bf16[544,768]{1,0:T(8,128)(2,1)S(1)}, bf16[544,768]{1,0:T(8,128)(2,1)}, u32[]{:S(2)}) copy-start(bf16[544,768]{1,0:T(8,128)(2,1)} %stage.1.refs_0_.refs_8_) | copy-start | bytes 2506756
  31.2 4.8 %collective-permute-start.6 = (bf16[544,768]{1,0:T(8,128)(2,1)S(1)}, bf16[544,768]{1,0:T(8,128)(2,1)S(1)}, u32[]{:S(2)}, u32[]{:S(2)}) collective-permute-start(bf16[544,768]{1,0:T(8,128)(2,1)S(1)} %collective-permute-done.refs_0_.refs_1_.refs_9_), channel_id=1, source_target_pairs={{0,8},{1,9},{2,10},{3,11},{4,12},{5,13},{6,14},{7,15},{8,0},{9,1},... | collective-permute-start | bytes 2506760 | tf_op jit(solution)/shard_map/ppermute | solution.py:60
  31.2 6.8 %collective-permute-start.7 = (bf16[544,768]{1,0:T(8,128)(2,1)S(1)}, bf16[544,768]{1,0:T(8,128)(2,1)S(1)}, u32[]{:S(2)}, u32[]{:S(2)}) collective-permute-start(bf16[544,768]{1,0:T(8,128)(2,1)S(1)} %collective-permute-done.1.refs_1_.refs_2_.refs_10_), channel_id=1, source_target_pairs={{0,8},{1,9},{2,10},{3,11},{4,12},{5,13},{6,14},{7,15},{8,0},{9,1},... | collective-permute-start | bytes 2506760 | tf_op jit(solution)/shard_map/ppermute | solution.py:60
  31.7 15.1 %collective-permute-start.5 = (bf16[544,768]{1,0:T(8,128)(2,1)S(1)}, bf16[544,768]{1,0:T(8,128)(2,1)S(1)}, u32[]{:S(2)}, u32[]{:S(2)}) collective-permute-start(bf16[544,768]{1,0:T(8,128)(2,1)S(1)} %collective-permute-done.refs_0_.refs_1_.refs_9_), channel_id=1, source_target_pairs={{0,16},{1,17},{2,18},{3,19},{4,20},{5,21},{6,22},{7,23},{8,56},{9,... | collective-permute-start | bytes 2506760 | tf_op jit(solution)/shard_map/ppermute | solution.py:60
  33.8 13.0 %collective-permute-start.10 = (bf16[128,384]{1,0:T(8,128)(2,1)S(1)}, bf16[128,384]{1,0:T(8,128)(2,1)S(1)}, u32[]{:S(2)}, u32[]{:S(2)}) collective-permute-start(bf16[128,384]{1,0:T(8,128)(2,1)S(1)} %get-tuple-element.81), channel_id=1, source_target_pairs={{0,3},{1,0},{2,1},{3,2},{4,7},{5,4},{6,5},{7,6},{8,9},{9,10},{10,1... | collective-permute-start | bytes 294920 | tf_op jit(solution)/shard_map/ppermute | solution.py:60
  34.2 12.5 %collective-permute-start.11 = (bf16[128,384]{1,0:T(8,128)(2,1)S(1)}, bf16[128,384]{1,0:T(8,128)(2,1)S(1)}, u32[]{:S(2)}, u32[]{:S(2)}) collective-permute-start(bf16[128,384]{1,0:T(8,128)(2,1)S(1)} %get-tuple-element.82), channel_id=1, source_target_pairs={{0,2},{1,3},{2,0},{3,1},{4,6},{5,7},{6,4},{7,5},{8,10},{9,11},{10,... | collective-permute-start | bytes 294920 | tf_op jit(solution)/shard_map/ppermute | solution.py:60
  36.0 10.8 %collective-permute-start.9 = (bf16[128,384]{1,0:T(8,128)(2,1)S(1)}, bf16[128,384]{1,0:T(8,128)(2,1)S(1)}, u32[]{:S(2)}, u32[]{:S(2)}) collective-permute-start(bf16[128,384]{1,0:T(8,128)(2,1)S(1)} %get-tuple-element.80), channel_id=1, source_target_pairs={{0,1},{1,2},{2,3},{3,0},{4,5},{5,6},{6,7},{7,4},{8,11},{9,8},{10,9... | collective-permute-start | bytes 294920 | tf_op jit(solution)/shard_map/ppermute | solution.py:60
  38.0 7.9 %copy-start.2 = (bf16[384,3072]{1,0:T(8,128)(2,1)S(1)}, bf16[384,3072]{1,0:T(8,128)(2,1)}, u32[]{:S(2)}) copy-start(bf16[384,3072]{1,0:T(8,128)(2,1)} %w.1) | copy-start | bytes 7077892
  45.9 2.7 %copy-start.1 = (bf16[544,768]{1,0:T(8,128)(2,1)S(1)}, bf16[544,768]{1,0:T(8,128)(2,1)}, u32[]{:S(2)}) copy-start(bf16[544,768]{1,0:T(8,128)(2,1)} %stage.1.refs_0_.refs_8_) | copy-start | bytes 2506756
  46.8 4.3 %collective-permute-start.12 = (bf16[544,768]{1,0:T(8,128)(2,1)S(1)}, bf16[544,768]{1,0:T(8,128)(2,1)S(1)}, u32[]{:S(2)}, u32[]{:S(2)}) collective-permute-start(bf16[544,768]{1,0:T(8,128)(2,1)S(1)} %collective-permute-done.5.refs_0_.refs_3_.refs_11_), channel_id=1, source_target_pairs={{0,8},{1,9},{2,10},{3,11},{4,12},{5,13},{6,14},{7,15},{8,0},{9,1},... | collective-permute-start | bytes 2506760 | tf_op jit(solution)/shard_map/ppermute | solution.py:60
  46.9 2.5 %collective-permute-start.13 = (bf16[128,384]{1,0:T(8,128)(2,1)S(1)}, bf16[128,384]{1,0:T(8,128)(2,1)S(1)}, u32[]{:S(2)}, u32[]{:S(2)}) collective-permute-start(bf16[128,384]{1,0:T(8,128)(2,1)S(1)} %get-tuple-element.84.refs_0_), channel_id=1, source_target_pairs={{0,8},{1,9},{2,10},{3,11},{4,12},{5,13},{6,14},{7,15},{8,0},{9,1},... | collective-permute-start | bytes 294920 | tf_op jit(solution)/shard_map/ppermute | solution.py:60
  47.4 3.3 %collective-permute-start.14 = (bf16[128,384]{1,0:T(8,128)(2,1)S(1)}, bf16[128,384]{1,0:T(8,128)(2,1)S(1)}, u32[]{:S(2)}, u32[]{:S(2)}) collective-permute-start(bf16[128,384]{1,0:T(8,128)(2,1)S(1)} %collective-permute-done.9.refs_1_), channel_id=1, source_target_pairs={{0,8},{1,9},{2,10},{3,11},{4,12},{5,13},{6,14},{7,15},{8,0},{9,1},... | collective-permute-start | bytes 294920 | tf_op jit(solution)/shard_map/ppermute | solution.py:60
  47.5 3.6 %collective-permute-start.15 = (bf16[128,384]{1,0:T(8,128)(2,1)S(1)}, bf16[128,384]{1,0:T(8,128)(2,1)S(1)}, u32[]{:S(2)}, u32[]{:S(2)}) collective-permute-start(bf16[128,384]{1,0:T(8,128)(2,1)S(1)} %collective-permute-done.10.refs_2_), channel_id=1, source_target_pairs={{0,8},{1,9},{2,10},{3,11},{4,12},{5,13},{6,14},{7,15},{8,0},{9,1},... | collective-permute-start | bytes 294920 | tf_op jit(solution)/shard_map/ppermute | solution.py:60
  47.9 3.2 %collective-permute-start.16 = (bf16[128,384]{1,0:T(8,128)(2,1)S(1)}, bf16[128,384]{1,0:T(8,128)(2,1)S(1)}, u32[]{:S(2)}, u32[]{:S(2)}) collective-permute-start(bf16[128,384]{1,0:T(8,128)(2,1)S(1)} %collective-permute-done.11.refs_3_), channel_id=1, source_target_pairs={{0,8},{1,9},{2,10},{3,11},{4,12},{5,13},{6,14},{7,15},{8,0},{9,1},... | collective-permute-start | bytes 294920 | tf_op jit(solution)/shard_map/ppermute | solution.py:60
  49.4 6.4 %collective-permute-start.18 = (bf16[128,768]{1,0:T(8,128)(2,1)S(1)}, bf16[128,768]{1,0:T(8,128)(2,1)S(1)}, u32[]{:S(2)}, u32[]{:S(2)}) collective-permute-start(bf16[128,768]{1,0:T(8,128)(2,1)S(1)} %prompt.1), channel_id=1, source_target_pairs={{0,64},{1,65},{2,66},{3,67},{4,68},{5,69},{6,70},{7,71},{8,72},{9,... | collective-permute-start | bytes 589832 | tf_op jit(solution)/shard_map/ppermute | solution.py:60
  50.7 19.4 %collective-permute-start.27 = (bf16[384,1536]{1,0:T(8,128)(2,1)S(1)}, bf16[384,1536]{1,0:T(8,128)(2,1)S(1)}, u32[]{:S(2)}, u32[]{:S(2)}) collective-permute-start(bf16[384,1536]{1,0:T(8,128)(2,1)S(1)} %get-tuple-element.112), channel_id=1, source_target_pairs={{0,8},{1,9},{2,10},{3,11},{4,12},{5,13},{6,14},{7,15},{8,0},{9,1},... | collective-permute-start | bytes 3538952 | tf_op jit(solution)/shard_map/ppermute | solution.py:60
  51.1 25.7 %collective-permute-start.28 = (bf16[384,1536]{1,0:T(8,128)(2,1)S(1)}, bf16[384,1536]{1,0:T(8,128)(2,1)S(1)}, u32[]{:S(2)}, u32[]{:S(2)}) collective-permute-start(bf16[384,1536]{1,0:T(8,128)(2,1)S(1)} %get-tuple-element.111.refs_9_), channel_id=1, source_target_pairs={{0,1},{1,2},{2,3},{3,0},{4,5},{5,6},{6,7},{7,4},{8,11},{9,8},{10,9... | collective-permute-start | bytes 3538952 | tf_op jit(solution)/shard_map/ppermute | solution.py:60
  54.0 5.3 %copy-start.7 = (s32[4]{0:T(128)S(1)}, s32[4]{0:T(128)}, u32[]{:S(2)}) copy-start(s32[4]{0:T(128)} %start_ref.1) | copy-start | bytes 52
  54.0 5.3 %copy-start.8 = (s32[4]{0:T(128)S(1)}, s32[4]{0:T(128)}, u32[]{:S(2)}) copy-start(s32[4]{0:T(128)} %length_ref.1) | copy-start | bytes 52
  54.0 11.0 %collective-permute-start.17 = (bf16[544,384]{1,0:T(8,128)(2,1)S(1)}, bf16[544,384]{1,0:T(8,128)(2,1)S(1)}, u32[]{:S(2)}, u32[]{:S(2)}) collective-permute-start(bf16[544,384]{1,0:T(8,128)(2,1)S(1)} %far_other.1), channel_id=1, source_target_pairs={{0,64},{1,65},{2,66},{3,67},{4,68},{5,69},{6,70},{7,71},{8,72},{9,... | collective-permute-start | bytes 1253384 | tf_op jit(solution)/shard_map/ppermute | solution.py:60
  55.7 3.5 %collective-permute-start.19 = (bf16[128,768]{1,0:T(8,128)(2,1)S(1)}, bf16[128,768]{1,0:T(8,128)(2,1)S(1)}, u32[]{:S(2)}, u32[]{:S(2)}) collective-permute-start(bf16[128,768]{1,0:T(8,128)(2,1)S(1)} %collective-permute-done.18.refs_16_), channel_id=1, source_target_pairs={{0,8},{1,9},{2,10},{3,11},{4,12},{5,13},{6,14},{7,15},{8,0},{9,1},... | collective-permute-start | bytes 589832 | tf_op jit(solution)/shard_map/ppermute | solution.py:60
  66.2 5.1 %collective-permute-start.20 = (bf16[128,384]{1,0:T(8,128)(2,1)S(1)}, bf16[128,384]{1,0:T(8,128)(2,1)S(1)}, u32[]{:S(2)}, u32[]{:S(2)}) collective-permute-start(bf16[128,384]{1,0:T(8,128)(2,1)S(1)} %get-tuple-element.107), channel_id=1, source_target_pairs={{0,1},{1,2},{2,3},{3,0},{4,5},{5,6},{6,7},{7,4},{8,11},{9,8},{10,9... | collective-permute-start | bytes 294920 | tf_op jit(solution)/shard_map/ppermute | solution.py:60
  66.3 7.0 %collective-permute-start.21 = (bf16[128,384]{1,0:T(8,128)(2,1)S(1)}, bf16[128,384]{1,0:T(8,128)(2,1)S(1)}, u32[]{:S(2)}, u32[]{:S(2)}) collective-permute-start(bf16[128,384]{1,0:T(8,128)(2,1)S(1)} %get-tuple-element.108), channel_id=1, source_target_pairs={{0,3},{1,0},{2,1},{3,2},{4,7},{5,4},{6,5},{7,6},{8,9},{9,10},{10,1... | collective-permute-start | bytes 294920 | tf_op jit(solution)/shard_map/ppermute | solution.py:60
  68.4 5.8 %collective-permute-start.22 = (bf16[128,384]{1,0:T(8,128)(2,1)S(1)}, bf16[128,384]{1,0:T(8,128)(2,1)S(1)}, u32[]{:S(2)}, u32[]{:S(2)}) collective-permute-start(bf16[128,384]{1,0:T(8,128)(2,1)S(1)} %get-tuple-element.109), channel_id=1, source_target_pairs={{0,2},{1,3},{2,0},{3,1},{4,6},{5,7},{6,4},{7,5},{8,10},{9,11},{10,... | collective-permute-start | bytes 294920 | tf_op jit(solution)/shard_map/ppermute | solution.py:60
  70.1 6.7 %collective-permute-start.23 = (bf16[128,384]{1,0:T(8,128)(2,1)S(1)}, bf16[128,384]{1,0:T(8,128)(2,1)S(1)}, u32[]{:S(2)}, u32[]{:S(2)}) collective-permute-start(bf16[128,384]{1,0:T(8,128)(2,1)S(1)} %get-tuple-element.106.refs_0_), channel_id=1, source_target_pairs={{0,8},{1,9},{2,10},{3,11},{4,12},{5,13},{6,14},{7,15},{8,0},{9,1},... | collective-permute-start | bytes 294920 | tf_op jit(solution)/shard_map/ppermute | solution.py:60
  71.3 5.5 %collective-permute-start.24 = (bf16[128,384]{1,0:T(8,128)(2,1)S(1)}, bf16[128,384]{1,0:T(8,128)(2,1)S(1)}, u32[]{:S(2)}, u32[]{:S(2)}) collective-permute-start(bf16[128,384]{1,0:T(8,128)(2,1)S(1)} %collective-permute-done.20.refs_1_), channel_id=1, source_target_pairs={{0,8},{1,9},{2,10},{3,11},{4,12},{5,13},{6,14},{7,15},{8,0},{9,1},... | collective-permute-start | bytes 294920 | tf_op jit(solution)/shard_map/ppermute | solution.py:60
  73.3 3.5 %collective-permute-start.25 = (bf16[128,384]{1,0:T(8,128)(2,1)S(1)}, bf16[128,384]{1,0:T(8,128)(2,1)S(1)}, u32[]{:S(2)}, u32[]{:S(2)}) collective-permute-start(bf16[128,384]{1,0:T(8,128)(2,1)S(1)} %collective-permute-done.21.refs_2_), channel_id=1, source_target_pairs={{0,8},{1,9},{2,10},{3,11},{4,12},{5,13},{6,14},{7,15},{8,0},{9,1},... | collective-permute-start | bytes 294920 | tf_op jit(solution)/shard_map/ppermute | solution.py:60
  74.2 3.5 %collective-permute-start.26 = (bf16[128,384]{1,0:T(8,128)(2,1)S(1)}, bf16[128,384]{1,0:T(8,128)(2,1)S(1)}, u32[]{:S(2)}, u32[]{:S(2)}) collective-permute-start(bf16[128,384]{1,0:T(8,128)(2,1)S(1)} %collective-permute-done.22.refs_3_), channel_id=1, source_target_pairs={{0,8},{1,9},{2,10},{3,11},{4,12},{5,13},{6,14},{7,15},{8,0},{9,1},... | collective-permute-start | bytes 294920 | tf_op jit(solution)/shard_map/ppermute | solution.py:60
  79.5 7.7 %collective-permute-start.29 = (bf16[64,1536]{1,0:T(8,128)(2,1)S(1)}, bf16[64,1536]{1,0:T(8,128)(2,1)S(1)}, u32[]{:S(2)}, u32[]{:S(2)}) collective-permute-start(bf16[64,1536]{1,0:T(8,128)(2,1)S(1)} %get-tuple-element.114), channel_id=1, source_target_pairs={{0,4},{1,5},{2,6},{3,7},{4,0},{5,1},{6,2},{7,3},{8,12},{9,13},{10,... | collective-permute-start | bytes 589832 | tf_op jit(solution)/shard_map/ppermute | solution.py:60
  82.2 5.0 %collective-permute-start.30 = (bf16[64,1536]{1,0:T(8,128)(2,1)S(1)}, bf16[64,1536]{1,0:T(8,128)(2,1)S(1)}, u32[]{:S(2)}, u32[]{:S(2)}) collective-permute-start(bf16[64,1536]{1,0:T(8,128)(2,1)S(1)} %get-tuple-element.115), channel_id=1, source_target_pairs={{0,8},{1,9},{2,10},{3,11},{4,12},{5,13},{6,14},{7,15},{8,0},{9,1},... | collective-permute-start | bytes 589832 | tf_op jit(solution)/shard_map/ppermute | solution.py:60
  82.8 9.1 %collective-permute-start.31 = (bf16[64,1536]{1,0:T(8,128)(2,1)S(1)}, bf16[64,1536]{1,0:T(8,128)(2,1)S(1)}, u32[]{:S(2)}, u32[]{:S(2)}) collective-permute-start(bf16[64,1536]{1,0:T(8,128)(2,1)S(1)} %get-tuple-element.116), channel_id=1, source_target_pairs={{0,12},{1,13},{2,14},{3,15},{4,8},{5,9},{6,10},{7,11},{8,4},{9,5},... | collective-permute-start | bytes 589832 | tf_op jit(solution)/shard_map/ppermute | solution.py:60
